TPU v7x, 32 devices: a whole 2x2x4 slice. The times are simulated.
32 devices in a mesh: seq: 16 (over z, y, core), head: 2 (over x).
Axes of the slice: x: 2, y: 2, z: 4, core: 2. Of those that a mesh axis runs over, the one named last changes fastest.
Arguments:
- queries: bfloat16 [6144, 768], P('seq', 'head'), as said below
- keys: bfloat16 [6144, 768], P('seq', 'head'), as said below
- values: bfloat16 [6144, 768], P('seq', 'head'), may hold values from -6 to 6
- image_tiles: int32 [5], replicated, may hold values from 1 to 21, 48 in all
Outputs:
- attended: bfloat16 [6144, 768], P(('seq', 'head'))
Inputs may be any that keep to these rules, and one draw needn't show every extreme that they name: `image_tiles`: the 5 images fill all 48 tiles in order; the longest holds exactly 21 tiles. `queries`: entries lie within -6 and 6. `keys`: entries lie within -6 and 6.
All inputs are finite; a program needn't handle non-finite values.
Results may differ from a plain program's by a relative error of at most 0.007.
Values may be sent and summed in bfloat16 or wider, within the bound.
No kernel may reach another device: no remote copies, remote signals or barrier semaphores. Data moves between devices by JAX's collectives and lax.ppermute only.
A program may use at most 64 MiB of HBM per device.

v0:
```python
import functools
import math

import jax
import jax.numpy as jnp
from jax import lax
from jax.experimental import pallas as pl
from jax.experimental.pallas import tpu as pltpu
from jax.sharding import PartitionSpec as P

HEAD_DIM = 128
TILE = 128
MOST_TILES = 21

LOWEST = -1e30
SCALE2 = math.log2(math.e) / math.sqrt(HEAD_DIM)
COST = 2

VMEM = pl.BlockSpec(memory_space=pltpu.VMEM)
SMEM = pl.BlockSpec(memory_space=pltpu.SMEM)
HBM = pl.BlockSpec(memory_space=pl.ANY)


def params():
    return pltpu.CompilerParams(vmem_limit_bytes=24 * 1024 * 1024)


def head_columns(h):
    return slice(h * HEAD_DIM, (h + 1) * HEAD_DIM)


def tile_rows(t):
    return slice(t * TILE, (t + 1) * TILE)


def image_bounds(tiles_ref, tile):
    first = jnp.int32(0)
    start, end = jnp.int32(0), jnp.int32(0)
    for i in range(tiles_ref.shape[0]):
        after = first + tiles_ref[i]
        inside = (tile >= first) & (tile < after)
        start = jnp.where(inside, first, start)
        end = jnp.where(inside, after, end)
        first = after
    return start, end


def meta_kernel(halves, tiles_ref, bounds_ref, far_ref):
    tiles = bounds_ref.shape[1] // TILE
    me = lax.axis_index("seq")
    bounds_ref[...] = jnp.zeros(bounds_ref.shape, jnp.int32)
    for half, owner in enumerate(halves(me)):
        for t in range(tiles):
            start, end = image_bounds(tiles_ref, owner * tiles + t)
            bounds_ref[2 * half : 2 * half + 1, tile_rows(t)] = jnp.full((1, TILE), start, jnp.int32)
            bounds_ref[2 * half + 1 : 2 * half + 2, tile_rows(t)] = jnp.full((1, TILE), end, jnp.int32)
    first = jnp.int32(0)
    far = jnp.int32(0)
    for i in range(tiles_ref.shape[0]):
        after = first + tiles_ref[i]
        levels = (after - 1) // (4 * tiles) - first // (4 * tiles)
        far = jnp.where(levels >= 2, 1, far)
        first = after
    far_ref[0] = far


def meta(halves, image_tiles, rows):
    bounds, far = pl.pallas_call(
        functools.partial(meta_kernel, halves),
        out_shape=[jax.ShapeDtypeStruct((8, rows), jnp.int32), jax.ShapeDtypeStruct((1,), jnp.int32)],
        in_specs=[SMEM],
        out_specs=[VMEM, SMEM],
        compiler_params=params(),
        cost_estimate=pl.CostEstimate(flops=COST * 2**28, bytes_accessed=0, transcendentals=0),
        name="meta",
    )(image_tiles)
    return bounds, far[0]


def pack_kernel(k_ref, v_ref, out_ref, held, sems):
    rows, columns = k_ref.shape
    tiles = rows // TILE
    copies = []
    for t in range(tiles):
        copies.append(pltpu.make_async_copy(v_ref.at[tile_rows(t)], held.at[tile_rows(t)], sems.at[2 * t]))
        copies.append(pltpu.make_async_copy(k_ref.at[tile_rows(t)], out_ref.at[tile_rows(2 * t)], sems.at[2 * t + 1]))
    for copy in copies:
        copy.start()
    for t in range(tiles):
        copies[2 * t].wait()
        for h in range(columns // HEAD_DIM):
            out_ref[tile_rows(2 * t + 1), head_columns(h)] = held[tile_rows(t), head_columns(h)].T
    for copy in copies[1::2]:
        copy.wait()


def pack(keys, values):
    rows, columns = keys.shape
    return pl.pallas_call(
        pack_kernel,
        out_shape=jax.ShapeDtypeStruct((2 * rows, columns), keys.dtype),
        in_specs=[HBM, HBM],
        out_specs=VMEM,
        scratch_shapes=[pltpu.VMEM(values.shape, values.dtype), pltpu.SemaphoreType.DMA((2 * rows // TILE,))],
        name="pack",
    )(keys, values)


def corner_kernel(block_ref, out_ref):
    skip = pl.multiple_of((lax.axis_index("seq") % 2) * 2 * TILE, 2 * TILE)
    out_ref[...] = block_ref[pl.ds(skip, out_ref.shape[0])]


def corner_of(block):
    return pl.pallas_call(
        corner_kernel,
        out_shape=jax.ShapeDtypeStruct((block.shape[0] - 2 * TILE, block.shape[1]), block.dtype),
        in_specs=[VMEM],
        out_specs=VMEM,
        compiler_params=params(),
        name="corner",
    )(block)


def attend_kernel(which, places, arrays, fresh, bounds_ref, *refs):
    halves = len(which)
    q_refs, refs = refs[:halves], refs[halves:]
    array_refs, refs = refs[: len(arrays)], refs[len(arrays) :]
    old_refs, refs = (None, refs) if fresh else (refs[:halves], refs[halves:])
    new_refs, (held_q, held, state) = refs[:halves], refs[halves:]
    rows, columns = q_refs[0].shape
    tiles = rows // TILE
    count = held.shape[1] // 2 // TILE
    heads = columns // HEAD_DIM
    me = lax.axis_index("seq")

    for half in range(halves):
        held_q[half] = q_refs[half][...]
        if fresh:
            state[half, :columns] = jnp.zeros((columns, rows), jnp.float32)
            state[half, columns : columns + heads] = jnp.full((heads, rows), LOWEST, jnp.float32)
            state[half, columns + heads :] = jnp.zeros((state.shape[1] - columns - heads, rows), jnp.float32)
        else:
            state[half] = old_refs[half][...]
    for slot, (array, shift) in enumerate(arrays):
        size = array_refs[array].shape[0]
        if size < held.shape[1]:
            held[slot] = jnp.zeros(held.shape[1:], held.dtype)
        at = 0 if shift is None else pl.multiple_of(shift(me), 2 * TILE)
        held[slot, pl.ds(at, size)] = array_refs[array][...]
    begins = [bounds_ref[2 * w, 0] for w in which]
    stops = [bounds_ref[2 * w + 1, rows - 1] for w in which]

    def chosen(at, options):
        return functools.reduce(lambda x, i: jnp.where(at == i, options[i], x), range(1, len(options)), options[0])

    def fold(half, slot, first):
        row = 2 * (which[0] + half * (which[-1] - which[0]) // max(len(which) - 1, 1))
        low = bounds_ref[pl.ds(row, 1), :]
        high = bounds_ref[pl.ds(row + 1, 1), :]
        off = [
            jnp.where((first + j >= low) & (first + j < high), 0.0, -LOWEST).astype(jnp.float32)
            for j in range(count)
        ]
        for h in range(heads):
            own = head_columns(h)
            scores = lax.dot_general(
                jnp.concatenate([held[slot, tile_rows(2 * j), own] for j in range(count)], axis=0),
                held_q[half, :, own],
                (((1,), (1,)), ((), ())),
                preferred_element_type=jnp.float32,
            )
            max_at, total_at = pl.ds(columns + h, 1), pl.ds(columns + heads + h, 1)
            factors, rounded, totals, maxima = [], [], [], []
            for t in range(tiles):
                lanes = tile_rows(t)
                parts = [scores[tile_rows(j), lanes] for j in range(count)]
                old_max = state[half, max_at, lanes]
                new_max = old_max
                for j in range(count):
                    new_max = jnp.maximum(new_max, jnp.max(parts[j], axis=0, keepdims=True) - off[j][:, lanes])
                scaled = new_max * SCALE2
                weights = [jnp.exp2(parts[j] * SCALE2 - (scaled + off[j][:, lanes])) for j in range(count)]
                factors.append(jnp.exp2((old_max - new_max) * SCALE2))
                totals.append(jnp.sum(functools.reduce(jnp.add, weights), axis=0, keepdims=True))
                maxima.append(new_max)
                rounded.append(jnp.concatenate([w.astype(jnp.bfloat16) for w in weights], axis=0))
            factor = jnp.concatenate(factors, axis=1)
            update = jnp.dot(
                jnp.concatenate([held[slot, tile_rows(2 * j + 1), own] for j in range(count)], axis=1),
                jnp.concatenate(rounded, axis=1),
                preferred_element_type=jnp.float32,
            )
            state[half, own] = state[half, own] * factor + update
            state[half, max_at] = jnp.concatenate(maxima, axis=1)
            state[half, total_at] = state[half, total_at] * factor + jnp.concatenate(totals, axis=1)

    @pl.loop(0, halves * len(places))
    def _(unit):
        half, slot = unit // len(places), unit % len(places)
        first = chosen(slot, [place(me) for place in places])

        @pl.when((first < chosen(half, stops)) & (first + count > chosen(half, begins)))
        def _():
            fold(half, slot, first)

    for half in range(halves):
        new_refs[half][...] = state[half]


def attend(bounds, queries, blocks, places, states, which=None, shifts=None):
    which = list(range(len(queries))) if which is None else which
    queries, states = [queries[w] for w in which], [states[w] for w in which] if states else []
    halves = len(which)
    rows, columns = queries[0].shape
    depth = blocks[0].shape[0]
    heads = columns // HEAD_DIM
    shape = jax.ShapeDtypeStruct((columns + -(-2 * heads // 8) * 8, rows), jnp.float32)
    arrays = list(enumerate(shifts or [None] * len(blocks)))
    pairs = halves * (rows // TILE) * heads * len(blocks) * (depth // 2 // TILE)
    return pl.pallas_call(
        functools.partial(attend_kernel, which, places, arrays, not states),
        out_shape=[shape] * halves,
        in_specs=[VMEM] * (1 + halves + len(blocks) + len(states)),
        out_specs=[VMEM] * halves,
        scratch_shapes=[
            pltpu.VMEM((halves, rows, columns), queries[0].dtype),
            pltpu.VMEM((len(blocks), depth, columns), blocks[0].dtype),
            pltpu.VMEM((halves,) + shape.shape, jnp.float32),
        ],
        compiler_params=params(),
        cost_estimate=pl.CostEstimate(
            flops=COST * pairs * 4 * TILE * TILE * HEAD_DIM,
            bytes_accessed=2 * len(blocks) * depth * columns + 4 * halves * rows * columns,
            transcendentals=pairs * TILE * TILE,
        ),
        name="attend",
    )(bounds, *queries, *blocks, *states)


def merged(states, columns):
    heads = columns // HEAD_DIM
    for h in range(heads):
        maxima = [ref[columns + h : columns + h + 1] for ref in states]
        totals = [ref[columns + heads + h : columns + heads + h + 1] for ref in states]
        largest = functools.reduce(jnp.maximum, maxima)
        factors = [jnp.exp2((m - largest) * SCALE2) for m in maxima]
        total = functools.reduce(jnp.add, [f * t for f, t in zip(factors, totals)])
        parts = [ref[head_columns(h)] * (f / total) for ref, f in zip(states, factors)]
        yield head_columns(h), functools.reduce(jnp.add, parts).T


def finish_kernel(*refs):
    out_ref = refs[-1]
    for own, done in merged(refs[:-1], out_ref.shape[1]):
        out_ref[:, own] = done.astype(out_ref.dtype)


def finish(states, rows, columns):
    return pl.pallas_call(
        finish_kernel,
        out_shape=jax.ShapeDtypeStruct((rows, columns), jnp.bfloat16),
        in_specs=[VMEM] * len(states),
        out_specs=VMEM,
        compiler_params=params(),
        name="finish",
    )(*states)


def message_kernel(*refs):
    states, outs, held = refs[:4], refs[4:8], refs[8]
    rows = outs[0].shape[0] - 2 * 8
    columns = outs[0].shape[1]
    heads = columns // HEAD_DIM
    mine = lax.axis_index("head")
    for part in range(2):
        pair, (keep_ref, send_ref) = states[2 * part : 2 * part + 2], outs[2 * part : 2 * part + 2]
        logs = []
        for h in range(heads):
            maxima = [ref[columns + h : columns + h + 1] for ref in pair]
            totals = [ref[columns + heads + h : columns + heads + h + 1] for ref in pair]
            largest = jnp.maximum(*maxima)
            factors = [jnp.exp2((m - largest) * SCALE2) for m in maxima]
            total = factors[0] * totals[0] + factors[1] * totals[1]
            some = jnp.where(total > 0, total, 1.0)
            scale = [f / some for f in factors]
            own = head_columns(h)
            held[:, own] = (pair[0][own] * scale[0] + pair[1][own] * scale[1]).T.astype(held.dtype)
            left = jnp.where(total > 0, largest * SCALE2 + jnp.log2(some), LOWEST)
            for _ in range(3):
                summand = left.astype(held.dtype).astype(jnp.float32)
                logs.append(summand)
                left = left - summand
        logs = jnp.concatenate(logs + [jnp.zeros((2 * 8 - len(logs), held.shape[0]), jnp.float32)], axis=0)
        later = pltpu.roll(logs, rows, 1)
        for ref, which in ((send_ref, 1 - mine), (keep_ref, mine)):
            ref[:rows] = held[pl.ds(pl.multiple_of(which * rows, 2 * 8), rows), :]
            ref[rows:] = jnp.where(which == 0, logs, later).astype(ref.dtype)


def messages(mine, peers):
    rows, columns = mine[0].shape[1], mine[0].shape[0] // HEAD_DIM * HEAD_DIM
    shape = jax.ShapeDtypeStruct((rows // 2 + 2 * 8, columns), jnp.bfloat16)
    return pl.pallas_call(
        message_kernel,
        out_shape=[shape] * 4,
        in_specs=[VMEM] * 4,
        out_specs=[VMEM] * 4,
        scratch_shapes=[pltpu.VMEM((rows, columns), jnp.bfloat16)],
        compiler_params=params(),
        name="message",
    )(*mine, *peers)


def settle_kernel(*refs):
    parts, out_ref, logs = refs[:4], refs[4], refs[5]
    rows, columns = out_ref.shape[0], parts[0].shape[1]
    heads = columns // HEAD_DIM
    mine = lax.axis_index("head")
    logs[...] = jnp.zeros(logs.shape, jnp.float32)
    for i, ref in enumerate(parts):
        summands = ref[rows:].astype(jnp.float32)
        for h in range(heads):
            at = i * heads + h
            logs[at : at + 1] = functools.reduce(jnp.add, [summands[3 * h + n : 3 * h + n + 1] for n in range(3)])
    turned = logs[...].T[:rows]
    for side, base in ((0, mine), (1, 1 - mine)):
        for h in range(heads):
            both = [turned[:, at : at + 1] for at in (2 * side * heads + h, (2 * side + 1) * heads + h)]
            largest = jnp.maximum(*both)
            weights = [jnp.exp2(x - largest) for x in both]
            sums = [ref[:rows, head_columns(h)].astype(jnp.float32) for ref in parts[2 * side : 2 * side + 2]]
            total = weights[0] + weights[1]
            done = sums[0] * (weights[0] / total) + sums[1] * (weights[1] / total)
            at = pl.multiple_of(base * columns + h * HEAD_DIM, HEAD_DIM)
            out_ref[:, pl.ds(at, HEAD_DIM)] = done.astype(out_ref.dtype)


def settle(own, across, beside, diagonal):
    rows, columns = own.shape[0] - 2 * 8, own.shape[1]
    return pl.pallas_call(
        settle_kernel,
        out_shape=jax.ShapeDtypeStruct((rows, 2 * columns), own.dtype),
        in_specs=[VMEM] * 4,
        out_specs=VMEM,
        scratch_shapes=[pltpu.VMEM((TILE, columns), jnp.float32)],
        compiler_params=params(),
        name="settle",
    )(own, across, beside, diagonal)


def chip_pairs(mesh):
    places = [tuple(getattr(d, "coords", ())) for d in mesh.devices[:, 0]]
    count = len(places)
    if count % 4 or not places[0] or mesh.shape["head"] != 2:
        return False
    cores = all(places[i] == places[i + 1] for i in range(0, count, 2))
    level = all(places[i][2] == places[i + 3][2] for i in range(0, count, 4))
    climb = all(places[i][2] != places[i + 4][2] for i in range(0, count - 4))
    return cores and level and climb


def paired_shards(owner_count, queries, keys, values, image_tiles):
    rows, columns = queries.shape
    tiles = rows // TILE
    owners = range(owner_count)

    def flip(s):
        return 1 - 2 * ((s // 2) % 2)

    def core(s):
        return s % 2

    def moved(array, source, takes=lambda s: True):
        pairs = [(source(s), s) for s in owners if takes(s) and 0 <= source(s) < owner_count]
        return lax.ppermute(array, "seq", pairs)

    across = lambda s: s + 2 * flip(s)
    along = lambda s: s + 4 * flip(s)
    against = lambda s: s - 4 * flip(s)
    sibling = lambda s: s + 1 - 2 * core(s)
    inner = lambda s: core(s) == (1 - (s // 2) % 2)

    OWN = lambda s: s * tiles
    A1 = lambda s: along(s) * tiles
    B1 = lambda s: against(s) * tiles
    A2 = lambda s: (s + 8 * flip(s)) * tiles
    B2 = lambda s: jnp.where(inner(s), s - 8 * flip(s), -owner_count) * tiles

    peers = moved(queries, across)
    block = pack(keys, values)
    a1, b1 = moved(block, along), moved(block, against)
    level = (queries, moved(queries, sibling), peers, moved(peers, sibling))
    bounds, far = meta(lambda s: [s, sibling(s), across(s), sibling(across(s))], image_tiles, rows)
    fold = functools.partial(attend, bounds, level)
    states = fold([block], [OWN], [], which=[0, 1]) + fold([block], [OWN], [], which=[2, 3])

    def merge(blocks, places, states, shifts=None):
        beside, diagonal = fold(blocks, places, states, which=[1, 3], shifts=shifts)
        beside, diagonal = moved(beside, sibling), moved(diagonal, sibling)
        mine, peer = fold(blocks, places, states, which=[0, 2], shifts=shifts)
        keep, over_x, over_y, over_both = messages([mine, beside], [peer, diagonal])
        pairs = [(2 * across(s) + 1 - x, 2 * s + x) for s in owners for x in range(2)]
        over_both = lax.ppermute(over_both, ("seq", "head"), pairs)
        over_y = moved(over_y, across)
        over_x = lax.ppermute(over_x, "head", [(0, 1), (1, 0)])
        return settle(keep, over_y, over_x, over_both)

    def near_only(a1, b1, states):
        return merge([a1, b1], [A1, B1], states)

    def both_ways(a1, b1, states):
        a2, b2 = moved(a1, along), moved(corner_of(b1), against, inner)
        states = fold([a1, b1], [A1, B1], states)
        return merge([a2, b2], [A2, B2], states, [None, lambda s: 2 * TILE * core(s)])

    return lax.cond(far > 0, both_ways, near_only, a1, b1, states)


def ring_shards(owner_count, queries, keys, values, image_tiles):
    rows, columns = queries.shape
    tiles = rows // TILE
    reach = min(owner_count - 1, -(-(MOST_TILES - 1) // tiles))
    block = pack(keys, values)
    bounds, _ = meta(lambda s: [s], image_tiles, rows)
    fold = functools.partial(attend, bounds, (queries,))
    up = [(i, i + 1) for i in range(owner_count - 1)]
    down = [(i + 1, i) for i in range(owner_count - 1)]
    below = above = block
    states = []
    held, places = [block], [lambda s: s * tiles]
    for k in range(1, reach + 1):
        below = lax.ppermute(below, "seq", up)
        above = lax.ppermute(above, "seq", down)
        states = fold(held, places, states)
        held, places = [below, above], [lambda s, k=k: (s - k) * tiles, lambda s, k=k: (s + k) * tiles]
    attended = finish(fold(held, places, states), rows, columns)
    return lax.all_to_all(attended, "head", split_axis=0, concat_axis=1, tiled=True)


def solution(mesh):
    owner_count = mesh.shape["seq"]
    plan = paired_shards if chip_pairs(mesh) else ring_shards
    placed = (P("seq", "head"), P("seq", "head"), P("seq", "head"), P())
    return jax.shard_map(
        functools.partial(plan, owner_count),
        mesh=mesh,
        in_specs=placed,
        out_specs=P(("seq", "head"), None),
        check_vma=False,
    )
```

profile of v0, /device:TPU:0, one launch (start us, length us, event | category | flops | bytes accessed | tf_op | source)
XLA Modules:
  0.0 44.8 jit_solution(4711091045925839488)
XLA Ops:
  0.0 0.0 copy-start.3
  0.0 0.0 copy-start.1
  0.0 3.0 %collective-permute-start.12 = (bf16[384,384]{1,0:T(8,128)(2,1)}, bf16[384,384]{1,0:T(8,128)(2,1)S(1)}, u32[]{:S(2)}, u32[]{:S(2)}) collective-permute-start(bf16[384,384]{1,0:T(8,128)(2,1)} %refs_0_.1), channel_id=1, source_target_pairs={{4,0},{6,2},{0,4},{2,6},{12,8},{14,10},{8,12},{10,14},{20,16},{22,... | collective-permute-start | bytes 884744 | tf_op jit(solution)/shard_map/ppermute | solution.py:376
  3.0 2.0 %pack.1.refs_2_ = bf16[768,384]{1,0:T(8,128)(2,1)} custom-call(bf16[384,384]{1,0:T(8,128)(2,1)} %k_ref.1, bf16[384,384]{1,0:T(8,128)(2,1)} %v_ref.1), custom_call_target="tpu_custom_call" | custom-call | tf_op jit(solution)/shard_map/pack/pallas_call | solution.py:99
  5.0 0.0 copy-start
  5.0 3.6 %collective-permute-start.14 = (bf16[768,384]{1,0:T(8,128)(2,1)}, bf16[768,384]{1,0:T(8,128)(2,1)S(1)}, u32[]{:S(2)}, u32[]{:S(2)}) collective-permute-start(bf16[768,384]{1,0:T(8,128)(2,1)} %pack.1.refs_2_), channel_id=1, source_target_pairs={{12,4},{14,6},{0,8},{2,10},{20,12},{22,14},{8,16},{10,18},{28,20},... | collective-permute-start | bytes 1769480 | tf_op jit(solution)/shard_map/ppermute | solution.py:376
  8.7 1.3 %collective-permute-start.13 = (bf16[768,384]{1,0:T(8,128)(2,1)}, bf16[768,384]{1,0:T(8,128)(2,1)S(1)}, u32[]{:S(2)}, u32[]{:S(2)}) collective-permute-start(bf16[768,384]{1,0:T(8,128)(2,1)} %pack.1.refs_2_), channel_id=1, source_target_pairs={{8,0},{10,2},{16,8},{18,10},{4,12},{6,14},{24,16},{26,18},{12,20},... | collective-permute-start | bytes 1769480 | tf_op jit(solution)/shard_map/ppermute | solution.py:376
  10.0 0.0 copy-done.3
  10.0 0.1 collective-permute-start.15
  10.1 0.2 collective-permute-done.12.refs_0_
  10.3 0.3 collective-permute-start.16
  10.6 0.0 copy-done.1
  10.6 1.2 %meta.1 = (s32[8,384]{1,0:T(8,128)S(1)}, s32[1]{0:T(128)}) custom-call(s32[5]{0:T(128)S(1)} %copy-done.1), custom_call_target="tpu_custom_call" | custom-call | flops 536870912 | tf_op jit(solution)/shard_map/meta/pallas_call | solution.py:68
  12.5 0.0 collective-permute-done.15.refs_1_
  12.5 0.0 copy-done
  12.5 2.8 %attend.12 = (f32[392,384]{1,0:T(8,128)S(1)}, f32[392,384]{1,0:T(8,128)S(1)}) custom-call(s32[8,384]{1,0:T(8,128)S(1)} %get-tuple-element.101.bounds_ref, bf16[384,384]{1,0:T(8,128)(2,1)S(1)} %copy-done.3, bf16[384,384]{1,0:T(8,128)(2,1)S(1)} %collective-permute-done.15.refs_1_, bf16[768,384]{1,0:T(8,128)(2,1)S(1)} %copy-done), custom_call_target="tpu_custom_call" | custom-call | flops 905969664 | bytes 1769472 | tf_op jit(solution)/shard_map/attend/pallas_call | solution.py:221
  15.2 0.0 collective-permute-done.16.refs_1_
  15.3 2.8 %attend.13 = (f32[392,384]{1,0:T(8,128)S(1)}, f32[392,384]{1,0:T(8,128)S(1)}) custom-call(s32[8,384]{1,0:T(8,128)S(1)} %get-tuple-element.101.bounds_ref, bf16[384,384]{1,0:T(8,128)(2,1)S(1)} %collective-permute-done.12.refs_0_, bf16[384,384]{1,0:T(8,128)(2,1)S(1)} %collective-permute-done.16.refs_1_, bf16[768,384]{1,0:T(8,128)(2,1)S(1)} %copy-done), custom_call_target="tpu_custom_call" | custom-call | flops 905969664 | bytes 1769472 | tf_op jit(solution)/shard_map/attend/pallas_call | solution.py:221
  18.0 3.2 %collective-permute-done.14 = bf16[768,384]{1,0:T(8,128)(2,1)S(1)} collective-permute-done((bf16[768,384]{1,0:T(8,128)(2,1)}, bf16[768,384]{1,0:T(8,128)(2,1)S(1)}, u32[]{:S(2)}, u32[]{:S(2)}) %collective-permute-start.14) | collective-permute-done | bytes 589856 | tf_op jit(solution)/shard_map/ppermute | solution.py:376
  21.3 4.0 %collective-permute-done.13 = bf16[768,384]{1,0:T(8,128)(2,1)S(1)} collective-permute-done((bf16[768,384]{1,0:T(8,128)(2,1)}, bf16[768,384]{1,0:T(8,128)(2,1)S(1)}, u32[]{:S(2)}, u32[]{:S(2)}) %collective-permute-start.13) | collective-permute-done | bytes 589856 | tf_op jit(solution)/shard_map/ppermute | solution.py:376
  25.3 18.7 %conditional.1 = (bf16[192,768]{1,0:T(8,128)(2,1)S(1)}) conditional(s32[]{:T(128)} %bitcast, (s32[8,384]{1,0:T(8,128)S(1)}, bf16[384,384]{1,0:T(8,128)(2,1)S(1)}, bf16[384,384]{1,0:T(8,128)(2,1)S(1)}, bf16[768,384]{1,0:T(8,128)(2,1)S(1)}, bf16[768,384]{1,0:T(8,128)(2,1)S(1)}, /*index=5*/f32[392,384]{1,0:T(8,128)S(1)}, f32[392,384]{1,0:T(8,128)S(1)}, ...), branch_computations={%region_0.0_spmd, %region_1.0_spmd} | conditional | flops 7247757312 | bytes 18923808 | solution.py:417
  25.3 2.9 %attend.8 = (f32[392,384]{1,0:T(8,128)S(1)}, f32[392,384]{1,0:T(8,128)S(1)}) custom-call(s32[8,384]{1,0:T(8,128)S(1)} %get-tuple-element.52.bounds_ref, bf16[384,384]{1,0:T(8,128)(2,1)S(1)} %get-tuple-element.60.refs_0_, bf16[384,384]{1,0:T(8,128)(2,1)S(1)} %get-tuple-element.61.refs_1_, bf16[768,384]{1,0:T(8,128)(2,1)S(1)} %get-tuple-element.55.refs_2_, ...), custom_call_target="tpu_custom_call" | custom-call | flops 1811939328 | bytes 2359296 | tf_op jit(solution)/shard_map/cond/branch_0_fun/attend/pallas_call | solution.py:221
  28.2 0.1 collective-permute-start
  28.3 0.5 %collective-permute-start.1 = (f32[392,384]{1,0:T(8,128)S(1)}, f32[392,384]{1,0:T(8,128)S(1)}, u32[]{:S(2)}, u32[]{:S(2)}) collective-permute-start(f32[392,384]{1,0:T(8,128)S(1)} %get-tuple-element.66), channel_id=1, source_target_pairs={{2,0},{0,2},{6,4},{4,6},{10,8},{8,10},{14,12},{12,14},{18,16},{16,... | collective-permute-start | bytes 1806344 | tf_op jit(solution)/shard_map/cond/branch_0_fun/ppermute | solution.py:376
  28.8 2.9 %attend.7 = (f32[392,384]{1,0:T(8,128)S(1)}, f32[392,384]{1,0:T(8,128)S(1)}) custom-call(s32[8,384]{1,0:T(8,128)S(1)} %get-tuple-element.52.bounds_ref, bf16[384,384]{1,0:T(8,128)(2,1)S(1)} %get-tuple-element.53.refs_0_, bf16[384,384]{1,0:T(8,128)(2,1)S(1)} %get-tuple-element.54.refs_1_, bf16[768,384]{1,0:T(8,128)(2,1)S(1)} %get-tuple-element.55.refs_2_, ...), custom_call_target="tpu_custom_call" | custom-call | flops 1811939328 | bytes 2359296 | tf_op jit(solution)/shard_map/cond/branch_0_fun/attend/pallas_call | solution.py:221
  31.7 0.0 collective-permute-done.refs_1_
  31.7 0.0 collective-permute-done.1.refs_3_
  31.7 0.5 %message.2 = (bf16[208,384]{1,0:T(8,128)(2,1)S(1)}, bf16[208,384]{1,0:T(8,128)(2,1)S(1)}, bf16[208,384]{1,0:T(8,128)(2,1)S(1)}, bf16[208,384]{1,0:T(8,128)(2,1)S(1)}) custom-call(f32[392,384]{1,0:T(8,128)S(1)} %get-tuple-element.59.refs_0_, f32[392,384]{1,0:T(8,128)S(1)} %collective-permute-done.refs_1_, f32[392,384]{1,0:T(8,128)S(1)} %get-tuple-element.65.refs_2_, ...), custom_call_target="tpu_custom_call" | custom-call | tf_op jit(solution)/shard_map/cond/branch_0_fun/message/pallas_call | solution.py:304
  32.2 0.1 collective-permute-start.2
  32.3 1.5 %collective-permute-start.3 = (bf16[208,384]{1,0:T(8,128)(2,1)S(1)}, bf16[208,384]{1,0:T(8,128)(2,1)S(1)}, u32[]{:S(2)}, u32[]{:S(2)}) collective-permute-start(bf16[208,384]{1,0:T(8,128)(2,1)S(1)} %get-tuple-element.69), channel_id=1, source_target_pairs={{0,1},{1,0},{2,3},{3,2},{4,5},{5,4},{6,7},{7,6},{8,9},{9,8},{10,11... | collective-permute-start | bytes 479240 | tf_op jit(solution)/shard_map/cond/branch_0_fun/ppermute | solution.py:406
  33.8 1.9 %collective-permute-start.4 = (bf16[208,384]{1,0:T(8,128)(2,1)S(1)}, bf16[208,384]{1,0:T(8,128)(2,1)S(1)}, u32[]{:S(2)}, u32[]{:S(2)}) collective-permute-start(bf16[208,384]{1,0:T(8,128)(2,1)S(1)} %get-tuple-element.70), channel_id=1, source_target_pairs={{5,0},{4,1},{7,2},{6,3},{1,4},{0,5},{3,6},{2,7},{13,8},{12,9},{15,... | collective-permute-start | bytes 479240 | tf_op jit(solution)/shard_map/cond/branch_0_fun/ppermute | solution.py:404
  35.8 2.6 %collective-permute-done.2.refs_1_ = bf16[208,384]{1,0:T(8,128)(2,1)S(1)} collective-permute-done((bf16[208,384]{1,0:T(8,128)(2,1)S(1)}, bf16[208,384]{1,0:T(8,128)(2,1)S(1)}, u32[]{:S(2)}, u32[]{:S(2)}) %collective-permute-start.2) | collective-permute-done | bytes 159776 | tf_op jit(solution)/shard_map/cond/branch_0_fun/ppermute | solution.py:376
  38.4 0.9 %collective-permute-done.3.refs_2_ = bf16[208,384]{1,0:T(8,128)(2,1)S(1)} collective-permute-done((bf16[208,384]{1,0:T(8,128)(2,1)S(1)}, bf16[208,384]{1,0:T(8,128)(2,1)S(1)}, u32[]{:S(2)}, u32[]{:S(2)}) %collective-permute-start.3) | collective-permute-done | bytes 159776 | tf_op jit(solution)/shard_map/cond/branch_0_fun/ppermute | solution.py:406
  39.3 3.7 %collective-permute-done.4.refs_3_ = bf16[208,384]{1,0:T(8,128)(2,1)S(1)} collective-permute-done((bf16[208,384]{1,0:T(8,128)(2,1)S(1)}, bf16[208,384]{1,0:T(8,128)(2,1)S(1)}, u32[]{:S(2)}, u32[]{:S(2)}) %collective-permute-start.4) | collective-permute-done | bytes 159776 | tf_op jit(solution)/shard_map/cond/branch_0_fun/ppermute | solution.py:404
  43.0 0.8 %settle.2 = bf16[192,768]{1,0:T(8,128)(2,1)S(1)} custom-call(bf16[208,384]{1,0:T(8,128)(2,1)S(1)} %get-tuple-element.67.refs_0_, bf16[208,384]{1,0:T(8,128)(2,1)S(1)} %collective-permute-done.2.refs_1_, bf16[208,384]{1,0:T(8,128)(2,1)S(1)} %collective-permute-done.3.refs_2_, bf16[208,384]{1,0:T(8,128)(2,1)S(1)} %collective-permute-done.4.refs_3_), custom_call_target="tpu_custom_call" | custom-call | tf_op jit(solution)/shard_map/cond/branch_0_fun/settle/pallas_call | solution.py:341
  44.0 0.0 copy-start.2
  44.0 0.7 %copy-done.2 = bf16[192,768]{1,0:T(8,128)(2,1)} copy-done((bf16[192,768]{1,0:T(8,128)(2,1)}, bf16[192,768]{1,0:T(8,128)(2,1)S(1)}, u32[]{:S(2)}) %copy-start.2) | copy-done | bytes 294936
Async XLA Ops:
  0.0 10.0 %copy-start.3 = (bf16[384,384]{1,0:T(8,128)(2,1)S(1)}, bf16[384,384]{1,0:T(8,128)(2,1)}, u32[]{:S(2)}) copy-start(bf16[384,384]{1,0:T(8,128)(2,1)} %refs_0_.1) | copy-start | bytes 884740
  0.0 10.6 %copy-start.1 = (s32[5]{0:T(128)S(1)}, s32[5]{0:T(128)}, u32[]{:S(2)}) copy-start(s32[5]{0:T(128)} %tiles_ref.1) | copy-start | bytes 64
  0.0 10.3 %collective-permute-start.12 = (bf16[384,384]{1,0:T(8,128)(2,1)}, bf16[384,384]{1,0:T(8,128)(2,1)S(1)}, u32[]{:S(2)}, u32[]{:S(2)}) collective-permute-start(bf16[384,384]{1,0:T(8,128)(2,1)} %refs_0_.1), channel_id=1, source_target_pairs={{4,0},{6,2},{0,4},{2,6},{12,8},{14,10},{8,12},{10,14},{20,16},{22,... | collective-permute-start | bytes 884744 | tf_op jit(solution)/shard_map/ppermute | solution.py:376
  5.0 7.4 %copy-start = (bf16[768,384]{1,0:T(8,128)(2,1)S(1)}, bf16[768,384]{1,0:T(8,128)(2,1)}, u32[]{:S(2)}) copy-start(bf16[768,384]{1,0:T(8,128)(2,1)} %pack.1.refs_2_) | copy-start | bytes 1769476
  5.0 16.2 %collective-permute-start.14 = (bf16[768,384]{1,0:T(8,128)(2,1)}, bf16[768,384]{1,0:T(8,128)(2,1)S(1)}, u32[]{:S(2)}, u32[]{:S(2)}) collective-permute-start(bf16[768,384]{1,0:T(8,128)(2,1)} %pack.1.refs_2_), channel_id=1, source_target_pairs={{12,4},{14,6},{0,8},{2,10},{20,12},{22,14},{8,16},{10,18},{28,20},... | collective-permute-start | bytes 1769480 | tf_op jit(solution)/shard_map/ppermute | solution.py:376
  8.7 16.6 %collective-permute-start.13 = (bf16[768,384]{1,0:T(8,128)(2,1)}, bf16[768,384]{1,0:T(8,128)(2,1)S(1)}, u32[]{:S(2)}, u32[]{:S(2)}) collective-permute-start(bf16[768,384]{1,0:T(8,128)(2,1)} %pack.1.refs_2_), channel_id=1, source_target_pairs={{8,0},{10,2},{16,8},{18,10},{4,12},{6,14},{24,16},{26,18},{12,20},... | collective-permute-start | bytes 1769480 | tf_op jit(solution)/shard_map/ppermute | solution.py:376
  10.0 2.5 %collective-permute-start.15 = (bf16[384,384]{1,0:T(8,128)(2,1)S(1)}, bf16[384,384]{1,0:T(8,128)(2,1)S(1)}, u32[]{:S(2)}, u32[]{:S(2)}) collective-permute-start(bf16[384,384]{1,0:T(8,128)(2,1)S(1)} %copy-done.3), channel_id=1, source_target_pairs={{2,0},{0,2},{6,4},{4,6},{10,8},{8,10},{14,12},{12,14},{18,16},{16,... | collective-permute-start | bytes 884744 | tf_op jit(solution)/shard_map/ppermute | solution.py:376
  10.3 5.0 %collective-permute-start.16 = (bf16[384,384]{1,0:T(8,128)(2,1)S(1)}, bf16[384,384]{1,0:T(8,128)(2,1)S(1)}, u32[]{:S(2)}, u32[]{:S(2)}) collective-permute-start(bf16[384,384]{1,0:T(8,128)(2,1)S(1)} %collective-permute-done.12.refs_0_), channel_id=1, source_target_pairs={{2,0},{0,2},{6,4},{4,6},{10,8},{8,10},{14,12},{12,14},{18,16},{16,... | collective-permute-start | bytes 884744 | tf_op jit(solution)/shard_map/ppermute | solution.py:376
  28.2 3.5 %collective-permute-start = (f32[392,384]{1,0:T(8,128)S(1)}, f32[392,384]{1,0:T(8,128)S(1)}, u32[]{:S(2)}, u32[]{:S(2)}) collective-permute-start(f32[392,384]{1,0:T(8,128)S(1)} %get-tuple-element.64), channel_id=1, source_target_pairs={{2,0},{0,2},{6,4},{4,6},{10,8},{8,10},{14,12},{12,14},{18,16},{16,... | collective-permute-start | bytes 1806344 | tf_op jit(solution)/shard_map/cond/branch_0_fun/ppermute | solution.py:376
  28.3 3.4 %collective-permute-start.1 = (f32[392,384]{1,0:T(8,128)S(1)}, f32[392,384]{1,0:T(8,128)S(1)}, u32[]{:S(2)}, u32[]{:S(2)}) collective-permute-start(f32[392,384]{1,0:T(8,128)S(1)} %get-tuple-element.66), channel_id=1, source_target_pairs={{2,0},{0,2},{6,4},{4,6},{10,8},{8,10},{14,12},{12,14},{18,16},{16,... | collective-permute-start | bytes 1806344 | tf_op jit(solution)/shard_map/cond/branch_0_fun/ppermute | solution.py:376
  32.2 6.2 %collective-permute-start.2 = (bf16[208,384]{1,0:T(8,128)(2,1)S(1)}, bf16[208,384]{1,0:T(8,128)(2,1)S(1)}, u32[]{:S(2)}, u32[]{:S(2)}) collective-permute-start(bf16[208,384]{1,0:T(8,128)(2,1)S(1)} %get-tuple-element.68), channel_id=1, source_target_pairs={{4,0},{6,2},{0,4},{2,6},{12,8},{14,10},{8,12},{10,14},{20,16},{22,... | collective-permute-start | bytes 479240 | tf_op jit(solution)/shard_map/cond/branch_0_fun/ppermute | solution.py:376
  32.3 7.0 %collective-permute-start.3 = (bf16[208,384]{1,0:T(8,128)(2,1)S(1)}, bf16[208,384]{1,0:T(8,128)(2,1)S(1)}, u32[]{:S(2)}, u32[]{:S(2)}) collective-permute-start(bf16[208,384]{1,0:T(8,128)(2,1)S(1)} %get-tuple-element.69), channel_id=1, source_target_pairs={{0,1},{1,0},{2,3},{3,2},{4,5},{5,4},{6,7},{7,6},{8,9},{9,8},{10,11... | collective-permute-start | bytes 479240 | tf_op jit(solution)/shard_map/cond/branch_0_fun/ppermute | solution.py:406
  33.8 9.2 %collective-permute-start.4 = (bf16[208,384]{1,0:T(8,128)(2,1)S(1)}, bf16[208,384]{1,0:T(8,128)(2,1)S(1)}, u32[]{:S(2)}, u32[]{:S(2)}) collective-permute-start(bf16[208,384]{1,0:T(8,128)(2,1)S(1)} %get-tuple-element.70), channel_id=1, source_target_pairs={{5,0},{4,1},{7,2},{6,3},{1,4},{0,5},{3,6},{2,7},{13,8},{12,9},{15,... | collective-permute-start | bytes 479240 | tf_op jit(solution)/shard_map/cond/branch_0_fun/ppermute | solution.py:404
  44.0 0.7 %copy-start.2 = (bf16[192,768]{1,0:T(8,128)(2,1)}, bf16[192,768]{1,0:T(8,128)(2,1)S(1)}, u32[]{:S(2)}) copy-start(bf16[192,768]{1,0:T(8,128)(2,1)S(1)} %get-tuple-element.135) | copy-start | bytes 884740
where the time goes:
time: 44.2 us; the launch traced here: 44.8 us
  Pallas kernels  15.9 us (36%)
  waiting for transfers between devices  14.7 us (33%)
  starting transfers between devices  12.4 us (28%)
  between operations  0.77 us (2%)
  local copies, waits for them, and re-layouts  0.72 us (2%)
    pallas_call x4, Pallas kernels, attend(): pl.pallas_call(functools.partial(attend_kernel, which, places, arrays, no...  11.3 us
    ppermute x8, waiting for transfers between devices, moved(): return lax.ppermute(array, 'seq', pairs)  10.1 us
    ppermute x8, starting transfers between devices, moved(): return lax.ppermute(array, 'seq', pairs)  8.94 us
    ppermute x1, waiting for transfers between devices, merge(): over_both = lax.ppermute(over_both, ('seq', 'head'), pairs)  3.67 us
    pallas_call x1, Pallas kernels, pack(): pl.pallas_call(pack_kernel, out_shape=jax.ShapeDtypeStruct((2 * rows, col...  2.04 us
    ppermute x1, starting transfers between devices, merge(): over_both = lax.ppermute(over_both, ('seq', 'head'), pairs)  1.93 us
    ppermute x1, starting transfers between devices, merge(): over_x = lax.ppermute(over_x, 'head', [(0, 1), (1, 0)])  1.54 us
    pallas_call x1, Pallas kernels, meta(): pl.pallas_call(functools.partial(meta_kernel, halves), out_shape=[jax.Sha...  1.22 us
  transfers between devices with their start and end apart: 10, of which 6 were waited for; matrix products, arithmetic and copies ran while one was open for 0% of the time, Pallas kernels for 26%

commit v1 on v0

--- a/solution.py
+++ b/solution.py
@@ -106,20 +106,20 @@
     )(keys, values)
 
 
-def corner_kernel(block_ref, out_ref):
+def corner_kernel(block_ref, own_ref, out_ref):
     skip = pl.multiple_of((lax.axis_index("seq") % 2) * 2 * TILE, 2 * TILE)
     out_ref[...] = block_ref[pl.ds(skip, out_ref.shape[0])]
 
 
-def corner_of(block):
+def corner_of(block, own):
     return pl.pallas_call(
         corner_kernel,
         out_shape=jax.ShapeDtypeStruct((block.shape[0] - 2 * TILE, block.shape[1]), block.dtype),
-        in_specs=[VMEM],
+        in_specs=[VMEM, HBM],
         out_specs=VMEM,
         compiler_params=params(),
         name="corner",
-    )(block)
+    )(block, own)
 
 
 def attend_kernel(which, places, arrays, fresh, bounds_ref, *refs):
@@ -324,7 +324,7 @@
             at = i * heads + h
             logs[at : at + 1] = functools.reduce(jnp.add, [summands[3 * h + n : 3 * h + n + 1] for n in range(3)])
     turned = logs[...].T[:rows]
-    for side, base in ((0, mine), (1, 1 - mine)):
+    for side, base in ((0, 1 - mine), (1, mine)):
         for h in range(heads):
             both = [turned[:, at : at + 1] for at in (2 * side * heads + h, (2 * side + 1) * heads + h)]
             largest = jnp.maximum(*both)
@@ -336,7 +336,7 @@
             out_ref[:, pl.ds(at, HEAD_DIM)] = done.astype(out_ref.dtype)
 
 
-def settle(own, across, beside, diagonal):
+def settle(diagonal, beside, across, own):
     rows, columns = own.shape[0] - 2 * 8, own.shape[1]
     return pl.pallas_call(
         settle_kernel,
@@ -346,7 +346,7 @@
         scratch_shapes=[pltpu.VMEM((TILE, columns), jnp.float32)],
         compiler_params=params(),
         name="settle",
-    )(own, across, beside, diagonal)
+    )(diagonal, beside, across, own)
 
 
 def chip_pairs(mesh):
@@ -394,6 +394,7 @@
     bounds, far = meta(lambda s: [s, sibling(s), across(s), sibling(across(s))], image_tiles, rows)
     fold = functools.partial(attend, bounds, level)
     states = fold([block], [OWN], [], which=[0, 1]) + fold([block], [OWN], [], which=[2, 3])
+    states = fold([b1], [B1], states)
 
     def merge(blocks, places, states, shifts=None):
         beside, diagonal = fold(blocks, places, states, which=[1, 3], shifts=shifts)
@@ -404,17 +405,17 @@
         over_both = lax.ppermute(over_both, ("seq", "head"), pairs)
         over_y = moved(over_y, across)
         over_x = lax.ppermute(over_x, "head", [(0, 1), (1, 0)])
-        return settle(keep, over_y, over_x, over_both)
-
-    def near_only(a1, b1, states):
-        return merge([a1, b1], [A1, B1], states)
-
-    def both_ways(a1, b1, states):
-        a2, b2 = moved(a1, along), moved(corner_of(b1), against, inner)
-        states = fold([a1, b1], [A1, B1], states)
+        return settle(over_both, over_x, over_y, keep)
+
+    def near_only(block, a1, b1, states):
+        return merge([a1], [A1], states)
+
+    def both_ways(block, a1, b1, states):
+        a2, b2 = moved(a1, along), moved(corner_of(b1, block), against, inner)
+        states = fold([a1], [A1], states)
         return merge([a2, b2], [A2, B2], states, [None, lambda s: 2 * TILE * core(s)])
 
-    return lax.cond(far > 0, both_ways, near_only, a1, b1, states)
+    return lax.cond(far > 0, both_ways, near_only, block, a1, b1, states)
 
 
 def ring_shards(owner_count, queries, keys, values, image_tiles):

time: 44.2 us -> 59.9 us (1.36)
  the two profiles are of different devices: /device:TPU:0 before, /device:TPU:9 now
where the time goes in v1:
time: 59.9 us; the launch traced here: 59.7 us
  starting transfers between devices  20.8 us (35%)
  waiting for transfers between devices  19.4 us (32%)
  Pallas kernels  17.6 us (29%)
  between operations  0.76 us (1%)
  local copies, waits for them, and re-layouts  0.72 us (1%)
    ppermute x10, starting transfers between devices, moved(): return lax.ppermute(array, 'seq', pairs)  19.5 us
    pallas_call x6, Pallas kernels, attend(): pl.pallas_call(functools.partial(attend_kernel, which, places, arrays, no...  13.8 us
    ppermute x10, waiting for transfers between devices, moved(): return lax.ppermute(array, 'seq', pairs)  13.3 us
    ppermute x1, waiting for transfers between devices, merge(): over_both = lax.ppermute(over_both, ('seq', 'head'), pairs)  3.62 us
    ppermute x1, waiting for transfers between devices, merge(): over_x = lax.ppermute(over_x, 'head', [(0, 1), (1, 0)])  2.53 us
    ppermute x1, starting transfers between devices, merge(): over_x = lax.ppermute(over_x, 'head', [(0, 1), (1, 0)])  1.26 us
    pallas_call x1, Pallas kernels, pack(): pl.pallas_call(pack_kernel, out_shape=jax.ShapeDtypeStruct((2 * rows, col...  1.22 us
    pallas_call x1, Pallas kernels, meta(): pl.pallas_call(functools.partial(meta_kernel, halves), out_shape=[jax.Sha...  1.22 us
  transfers between devices with their start and end apart: 12, of which 9 were waited for; matrix products, arithmetic and copies ran while one was open for 0% of the time, Pallas kernels for 27%

profile of v1, /device:TPU:9, one launch (start us, length us, event | category | flops | bytes accessed | tf_op | source)
XLA Modules:
  0.0 59.7 jit_solution(2945526517246246919)
XLA Ops:
  0.0 0.0 copy-start.2
  0.0 0.0 copy-start
  0.0 1.2 %collective-permute-start.12 = (bf16[384,384]{1,0:T(8,128)(2,1)}, bf16[384,384]{1,0:T(8,128)(2,1)S(1)}, u32[]{:S(2)}, u32[]{:S(2)}) collective-permute-start(bf16[384,384]{1,0:T(8,128)(2,1)} %refs_0_.3), channel_id=1, source_target_pairs={{4,0},{6,2},{0,4},{2,6},{12,8},{14,10},{8,12},{10,14},{20,16},{22,... | collective-permute-start | bytes 884744 | tf_op jit(solution)/shard_map/ppermute | solution.py:376
  1.2 1.2 %pack.1.refs_2_ = bf16[768,384]{1,0:T(8,128)(2,1)S(1)} custom-call(bf16[384,384]{1,0:T(8,128)(2,1)} %k_ref.1, bf16[384,384]{1,0:T(8,128)(2,1)} %v_ref.1), custom_call_target="tpu_custom_call" | custom-call | tf_op jit(solution)/shard_map/pack/pallas_call | solution.py:99
  2.5 3.2 %collective-permute-start.16 = (bf16[768,384]{1,0:T(8,128)(2,1)S(1)}, bf16[768,384]{1,0:T(8,128)(2,1)S(1)}, u32[]{:S(2)}, u32[]{:S(2)}) collective-permute-start(bf16[768,384]{1,0:T(8,128)(2,1)S(1)} %pack.1.refs_2_), channel_id=1, source_target_pairs={{12,4},{14,6},{0,8},{2,10},{20,12},{22,14},{8,16},{10,18},{28,20},... | collective-permute-start | bytes 1769480 | tf_op jit(solution)/shard_map/ppermute | solution.py:376
  5.7 0.0 copy-done.2
  5.7 1.3 %collective-permute-start.14 = (bf16[384,384]{1,0:T(8,128)(2,1)S(1)}, bf16[384,384]{1,0:T(8,128)(2,1)S(1)}, u32[]{:S(2)}, u32[]{:S(2)}) collective-permute-start(bf16[384,384]{1,0:T(8,128)(2,1)S(1)} %copy-done.2), channel_id=1, source_target_pairs={{2,0},{0,2},{6,4},{4,6},{10,8},{8,10},{14,12},{12,14},{18,16},{16,... | collective-permute-start | bytes 884744 | tf_op jit(solution)/shard_map/ppermute | solution.py:376
  7.0 2.1 %collective-permute-start.13 = (bf16[768,384]{1,0:T(8,128)(2,1)S(1)}, bf16[768,384]{1,0:T(8,128)(2,1)S(1)}, u32[]{:S(2)}, u32[]{:S(2)}) collective-permute-start(bf16[768,384]{1,0:T(8,128)(2,1)S(1)} %pack.1.refs_2_), channel_id=1, source_target_pairs={{8,0},{10,2},{16,8},{18,10},{4,12},{6,14},{24,16},{26,18},{12,20},... | collective-permute-start | bytes 1769480 | tf_op jit(solution)/shard_map/ppermute | solution.py:376
  9.1 0.0 collective-permute-done.12.refs_0_.refs_2_
  9.1 0.5 collective-permute-start.15
  9.6 0.0 copy-done
  9.6 1.2 %meta.1 = (s32[8,384]{1,0:T(8,128)S(1)}, s32[1]{0:T(128)}) custom-call(s32[5]{0:T(128)S(1)} %copy-done), custom_call_target="tpu_custom_call" | custom-call | flops 536870912 | tf_op jit(solution)/shard_map/meta/pallas_call | solution.py:68
  11.5 0.0 collective-permute-done.14.refs_1_
  11.5 2.8 %attend.13 = (f32[392,384]{1,0:T(8,128)S(1)}, f32[392,384]{1,0:T(8,128)S(1)}) custom-call(s32[8,384]{1,0:T(8,128)S(1)} %get-tuple-element.105.bounds_ref, bf16[384,384]{1,0:T(8,128)(2,1)S(1)} %copy-done.2, bf16[384,384]{1,0:T(8,128)(2,1)S(1)} %collective-permute-done.14.refs_1_, bf16[768,384]{1,0:T(8,128)(2,1)S(1)} %pack.1.refs_2_), custom_call_target="tpu_custom_call" | custom-call | flops 905969664 | bytes 1769472 | tf_op jit(solution)/shard_map/attend/pallas_call | solution.py:221
  14.3 0.0 collective-permute-done.15.refs_1_.refs_3_
  14.3 2.8 %attend.14 = (f32[392,384]{1,0:T(8,128)S(1)}, f32[392,384]{1,0:T(8,128)S(1)}) custom-call(s32[8,384]{1,0:T(8,128)S(1)} %get-tuple-element.105.bounds_ref, bf16[384,384]{1,0:T(8,128)(2,1)S(1)} %collective-permute-done.12.refs_0_.refs_2_, bf16[384,384]{1,0:T(8,128)(2,1)S(1)} %collective-permute-done.15.refs_1_.refs_3_, bf16[768,384]{1,0:T(8,128)(2,1)S(1)} %pack.1.refs_2_), custom_call_target="tpu_custom_call" | custom-call | flops 905969664 | bytes 1769472 | tf_op jit(solution)/shard_map/attend/pallas_call | solution.py:221
  17.1 1.2 %collective-permute-done.16.refs_4_ = bf16[768,384]{1,0:T(8,128)(2,1)S(1)} collective-permute-done((bf16[768,384]{1,0:T(8,128)(2,1)S(1)}, bf16[768,384]{1,0:T(8,128)(2,1)S(1)}, u32[]{:S(2)}, u32[]{:S(2)}) %collective-permute-start.16) | collective-permute-done | bytes 589856 | tf_op jit(solution)/shard_map/ppermute | solution.py:376
  18.2 3.0 %attend.15 = (f32[392,384]{1,0:T(8,128)S(1)}, f32[392,384]{1,0:T(8,128)S(1)}, f32[392,384]{1,0:T(8,128)S(1)}, f32[392,384]{1,0:T(8,128)S(1)}) custom-call(s32[8,384]{1,0:T(8,128)S(1)} %get-tuple-element.105.bounds_ref, bf16[384,384]{1,0:T(8,128)(2,1)S(1)} %copy-done.2, bf16[384,384]{1,0:T(8,128)(2,1)S(1)} %collective-permute-done.14.refs_1_, ...), custom_call_target="tpu_custom_call" | custom-call | flops 1811939328 | bytes 2949120 | tf_op jit(solution)/shard_map/attend/pallas_call | solution.py:221
  21.3 2.5 %collective-permute-done.13 = bf16[768,384]{1,0:T(8,128)(2,1)S(1)} collective-permute-done((bf16[768,384]{1,0:T(8,128)(2,1)S(1)}, bf16[768,384]{1,0:T(8,128)(2,1)S(1)}, u32[]{:S(2)}, u32[]{:S(2)}) %collective-permute-start.13) | collective-permute-done | bytes 589856 | tf_op jit(solution)/shard_map/ppermute | solution.py:376
  23.8 35.1 %conditional.1 = (bf16[192,768]{1,0:T(8,128)(2,1)S(1)}) conditional(s32[]{:T(128)} %bitcast, (s32[8,384]{1,0:T(8,128)S(1)}, bf16[384,384]{1,0:T(8,128)(2,1)S(1)}, bf16[384,384]{1,0:T(8,128)(2,1)S(1)}, bf16[768,384]{1,0:T(8,128)(2,1)S(1)}, f32[392,384]{1,0:T(8,128)S(1)}, /*index=5*/f32[392,384]{1,0:T(8,128)S(1)}, bf16[384,384]{1,0:T(8,128)(2,1)S(1)}, ...), branch_computations={%region_0.0_spmd, %region_1.0_spmd} | conditional | flops 5435817984 | bytes 18333984 | solution.py:418
  23.8 2.1 %collective-permute-start.5 = (bf16[768,384]{1,0:T(8,128)(2,1)S(1)}, bf16[768,384]{1,0:T(8,128)(2,1)S(1)}, u32[]{:S(2)}, u32[]{:S(2)}) collective-permute-start(bf16[768,384]{1,0:T(8,128)(2,1)S(1)} %get-tuple-element.73.refs_4_), channel_id=1, source_target_pairs={{8,0},{10,2},{16,8},{18,10},{4,12},{6,14},{24,16},{26,18},{12,20},... | collective-permute-start | bytes 1769480 | tf_op jit(solution)/shard_map/cond/branch_1_fun/ppermute | solution.py:376
  25.9 0.1 corner.1
  26.0 3.4 %collective-permute-start.6 = (bf16[512,384]{1,0:T(8,128)(2,1)S(1)}, bf16[512,384]{1,0:T(8,128)(2,1)S(1)}, u32[]{:S(2)}, u32[]{:S(2)}) collective-permute-start(bf16[512,384]{1,0:T(8,128)(2,1)S(1)} %corner.1), channel_id=1, source_target_pairs={{12,4},{2,10},{20,12},{10,18},{28,20},{18,26},{13,5},{3,11},{21,13... | collective-permute-start | bytes 1179656 | tf_op jit(solution)/shard_map/cond/branch_1_fun/ppermute | solution.py:376
  29.3 4.3 %attend.10 = (f32[392,384]{1,0:T(8,128)S(1)}, f32[392,384]{1,0:T(8,128)S(1)}, f32[392,384]{1,0:T(8,128)S(1)}, f32[392,384]{1,0:T(8,128)S(1)}) custom-call(s32[8,384]{1,0:T(8,128)S(1)} %get-tuple-element.70.bounds_ref, bf16[384,384]{1,0:T(8,128)(2,1)S(1)} %get-tuple-element.71.refs_0_, bf16[384,384]{1,0:T(8,128)(2,1)S(1)} %get-tuple-element.76.refs_1_.refs_0_, ...), custom_call_target="tpu_custom_call" | custom-call | flops 1811939328 | bytes 2949120 | tf_op jit(solution)/shard_map/cond/branch_1_fun/attend/pallas_call | solution.py:221
  33.6 1.2 %collective-permute-done.6.refs_3_ = bf16[512,384]{1,0:T(8,128)(2,1)S(1)} collective-permute-done((bf16[512,384]{1,0:T(8,128)(2,1)S(1)}, bf16[512,384]{1,0:T(8,128)(2,1)S(1)}, u32[]{:S(2)}, u32[]{:S(2)}) %collective-permute-start.6) | collective-permute-done | bytes 393248 | tf_op jit(solution)/shard_map/cond/branch_1_fun/ppermute | solution.py:376
  34.8 4.9 %collective-permute-done.5.refs_2_ = bf16[768,384]{1,0:T(8,128)(2,1)S(1)} collective-permute-done((bf16[768,384]{1,0:T(8,128)(2,1)S(1)}, bf16[768,384]{1,0:T(8,128)(2,1)S(1)}, u32[]{:S(2)}, u32[]{:S(2)}) %collective-permute-start.5) | collective-permute-done | bytes 589856 | tf_op jit(solution)/shard_map/cond/branch_1_fun/ppermute | solution.py:376
  39.8 0.5 attend.12
  40.2 4.2 %collective-permute-start.7 = (f32[392,384]{1,0:T(8,128)S(1)}, f32[392,384]{1,0:T(8,128)S(1)}, u32[]{:S(2)}, u32[]{:S(2)}) collective-permute-start(f32[392,384]{1,0:T(8,128)S(1)} %get-tuple-element.87), channel_id=1, source_target_pairs={{2,0},{0,2},{6,4},{4,6},{10,8},{8,10},{14,12},{12,14},{18,16},{16,... | collective-permute-start | bytes 1806344 | tf_op jit(solution)/shard_map/cond/branch_1_fun/ppermute | solution.py:376
  44.4 0.1 collective-permute-start.8
  44.5 0.5 attend.11
  45.0 1.1 %collective-permute-done.7.refs_1_ = f32[392,384]{1,0:T(8,128)S(1)} collective-permute-done((f32[392,384]{1,0:T(8,128)S(1)}, f32[392,384]{1,0:T(8,128)S(1)}, u32[]{:S(2)}, u32[]{:S(2)}) %collective-permute-start.7) | collective-permute-done | bytes 602144 | tf_op jit(solution)/shard_map/cond/branch_1_fun/ppermute | solution.py:376
  46.1 0.9 %collective-permute-done.8.refs_3_ = f32[392,384]{1,0:T(8,128)S(1)} collective-permute-done((f32[392,384]{1,0:T(8,128)S(1)}, f32[392,384]{1,0:T(8,128)S(1)}, u32[]{:S(2)}, u32[]{:S(2)}) %collective-permute-start.8) | collective-permute-done | bytes 602144 | tf_op jit(solution)/shard_map/cond/branch_1_fun/ppermute | solution.py:376
  47.0 0.5 message.3
  47.5 0.1 collective-permute-start.9
  47.6 1.3 %collective-permute-start.10 = (bf16[208,384]{1,0:T(8,128)(2,1)S(1)}, bf16[208,384]{1,0:T(8,128)(2,1)S(1)}, u32[]{:S(2)}, u32[]{:S(2)}) collective-permute-start(bf16[208,384]{1,0:T(8,128)(2,1)S(1)} %get-tuple-element.91), channel_id=1, source_target_pairs={{0,1},{1,0},{2,3},{3,2},{4,5},{5,4},{6,7},{7,6},{8,9},{9,8},{10,11... | collective-permute-start | bytes 479240 | tf_op jit(solution)/shard_map/cond/branch_1_fun/ppermute | solution.py:407
  48.8 1.4 %collective-permute-start.11 = (bf16[208,384]{1,0:T(8,128)(2,1)S(1)}, bf16[208,384]{1,0:T(8,128)(2,1)S(1)}, u32[]{:S(2)}, u32[]{:S(2)}) collective-permute-start(bf16[208,384]{1,0:T(8,128)(2,1)S(1)} %get-tuple-element.92), channel_id=1, source_target_pairs={{4,0},{6,2},{0,4},{2,6},{12,8},{14,10},{8,12},{10,14},{20,16},{22,... | collective-permute-start | bytes 479240 | tf_op jit(solution)/shard_map/cond/branch_1_fun/ppermute | solution.py:376
  50.2 3.6 %collective-permute-done.9.refs_0_ = bf16[208,384]{1,0:T(8,128)(2,1)S(1)} collective-permute-done((bf16[208,384]{1,0:T(8,128)(2,1)S(1)}, bf16[208,384]{1,0:T(8,128)(2,1)S(1)}, u32[]{:S(2)}, u32[]{:S(2)}) %collective-permute-start.9) | collective-permute-done | bytes 159776 | tf_op jit(solution)/shard_map/cond/branch_1_fun/ppermute | solution.py:405
  53.8 2.5 %collective-permute-done.10.refs_1_ = bf16[208,384]{1,0:T(8,128)(2,1)S(1)} collective-permute-done((bf16[208,384]{1,0:T(8,128)(2,1)S(1)}, bf16[208,384]{1,0:T(8,128)(2,1)S(1)}, u32[]{:S(2)}, u32[]{:S(2)}) %collective-permute-start.10) | collective-permute-done | bytes 159776 | tf_op jit(solution)/shard_map/cond/branch_1_fun/ppermute | solution.py:407
  56.3 1.6 %collective-permute-done.11.refs_2_ = bf16[208,384]{1,0:T(8,128)(2,1)S(1)} collective-permute-done((bf16[208,384]{1,0:T(8,128)(2,1)S(1)}, bf16[208,384]{1,0:T(8,128)(2,1)S(1)}, u32[]{:S(2)}, u32[]{:S(2)}) %collective-permute-start.11) | collective-permute-done | bytes 159776 | tf_op jit(solution)/shard_map/cond/branch_1_fun/ppermute | solution.py:376
  57.9 0.8 %settle.3 = bf16[192,768]{1,0:T(8,128)(2,1)S(1)} custom-call(bf16[208,384]{1,0:T(8,128)(2,1)S(1)} %collective-permute-done.9.refs_0_, bf16[208,384]{1,0:T(8,128)(2,1)S(1)} %collective-permute-done.10.refs_1_, bf16[208,384]{1,0:T(8,128)(2,1)S(1)} %collective-permute-done.11.refs_2_, bf16[208,384]{1,0:T(8,128)(2,1)S(1)} %get-tuple-element.93.refs_3_), custom_call_target="tpu_custom_call" | custom-call | tf_op jit(solution)/shard_map/cond/branch_1_fun/settle/pallas_call | solution.py:341
  58.9 0.0 copy-start.1
  58.9 0.7 %copy-done.1 = bf16[192,768]{1,0:T(8,128)(2,1)} copy-done((bf16[192,768]{1,0:T(8,128)(2,1)}, bf16[192,768]{1,0:T(8,128)(2,1)S(1)}, u32[]{:S(2)}) %copy-start.1) | copy-done | bytes 294936
Async XLA Ops:
  0.0 5.7 %copy-start.2 = (bf16[384,384]{1,0:T(8,128)(2,1)S(1)}, bf16[384,384]{1,0:T(8,128)(2,1)}, u32[]{:S(2)}) copy-start(bf16[384,384]{1,0:T(8,128)(2,1)} %refs_0_.3) | copy-start | bytes 884740
  0.0 9.6 %copy-start = (s32[5]{0:T(128)S(1)}, s32[5]{0:T(128)}, u32[]{:S(2)}) copy-start(s32[5]{0:T(128)} %tiles_ref.1) | copy-start | bytes 64
  0.0 9.1 %collective-permute-start.12 = (bf16[384,384]{1,0:T(8,128)(2,1)}, bf16[384,384]{1,0:T(8,128)(2,1)S(1)}, u32[]{:S(2)}, u32[]{:S(2)}) collective-permute-start(bf16[384,384]{1,0:T(8,128)(2,1)} %refs_0_.3), channel_id=1, source_target_pairs={{4,0},{6,2},{0,4},{2,6},{12,8},{14,10},{8,12},{10,14},{20,16},{22,... | collective-permute-start | bytes 884744 | tf_op jit(solution)/shard_map/ppermute | solution.py:376
  2.5 15.8 %collective-permute-start.16 = (bf16[768,384]{1,0:T(8,128)(2,1)S(1)}, bf16[768,384]{1,0:T(8,128)(2,1)S(1)}, u32[]{:S(2)}, u32[]{:S(2)}) collective-permute-start(bf16[768,384]{1,0:T(8,128)(2,1)S(1)} %pack.1.refs_2_), channel_id=1, source_target_pairs={{12,4},{14,6},{0,8},{2,10},{20,12},{22,14},{8,16},{10,18},{28,20},... | collective-permute-start | bytes 1769480 | tf_op jit(solution)/shard_map/ppermute | solution.py:376
  5.7 5.8 %collective-permute-start.14 = (bf16[384,384]{1,0:T(8,128)(2,1)S(1)}, bf16[384,384]{1,0:T(8,128)(2,1)S(1)}, u32[]{:S(2)}, u32[]{:S(2)}) collective-permute-start(bf16[384,384]{1,0:T(8,128)(2,1)S(1)} %copy-done.2), channel_id=1, source_target_pairs={{2,0},{0,2},{6,4},{4,6},{10,8},{8,10},{14,12},{12,14},{18,16},{16,... | collective-permute-start | bytes 884744 | tf_op jit(solution)/shard_map/ppermute | solution.py:376
  7.0 16.8 %collective-permute-start.13 = (bf16[768,384]{1,0:T(8,128)(2,1)S(1)}, bf16[768,384]{1,0:T(8,128)(2,1)S(1)}, u32[]{:S(2)}, u32[]{:S(2)}) collective-permute-start(bf16[768,384]{1,0:T(8,128)(2,1)S(1)} %pack.1.refs_2_), channel_id=1, source_target_pairs={{8,0},{10,2},{16,8},{18,10},{4,12},{6,14},{24,16},{26,18},{12,20},... | collective-permute-start | bytes 1769480 | tf_op jit(solution)/shard_map/ppermute | solution.py:376
  9.1 5.2 %collective-permute-start.15 = (bf16[384,384]{1,0:T(8,128)(2,1)S(1)}, bf16[384,384]{1,0:T(8,128)(2,1)S(1)}, u32[]{:S(2)}, u32[]{:S(2)}) collective-permute-start(bf16[384,384]{1,0:T(8,128)(2,1)S(1)} %collective-permute-done.12.refs_0_.refs_2_), channel_id=1, source_target_pairs={{2,0},{0,2},{6,4},{4,6},{10,8},{8,10},{14,12},{12,14},{18,16},{16,... | collective-permute-start | bytes 884744 | tf_op jit(solution)/shard_map/ppermute | solution.py:376
  23.8 15.9 %collective-permute-start.5 = (bf16[768,384]{1,0:T(8,128)(2,1)S(1)}, bf16[768,384]{1,0:T(8,128)(2,1)S(1)}, u32[]{:S(2)}, u32[]{:S(2)}) collective-permute-start(bf16[768,384]{1,0:T(8,128)(2,1)S(1)} %get-tuple-element.73.refs_4_), channel_id=1, source_target_pairs={{8,0},{10,2},{16,8},{18,10},{4,12},{6,14},{24,16},{26,18},{12,20},... | collective-permute-start | bytes 1769480 | tf_op jit(solution)/shard_map/cond/branch_1_fun/ppermute | solution.py:376
  26.0 8.8 %collective-permute-start.6 = (bf16[512,384]{1,0:T(8,128)(2,1)S(1)}, bf16[512,384]{1,0:T(8,128)(2,1)S(1)}, u32[]{:S(2)}, u32[]{:S(2)}) collective-permute-start(bf16[512,384]{1,0:T(8,128)(2,1)S(1)} %corner.1), channel_id=1, source_target_pairs={{12,4},{2,10},{20,12},{10,18},{28,20},{18,26},{13,5},{3,11},{21,13... | collective-permute-start | bytes 1179656 | tf_op jit(solution)/shard_map/cond/branch_1_fun/ppermute | solution.py:376
  40.2 5.9 %collective-permute-start.7 = (f32[392,384]{1,0:T(8,128)S(1)}, f32[392,384]{1,0:T(8,128)S(1)}, u32[]{:S(2)}, u32[]{:S(2)}) collective-permute-start(f32[392,384]{1,0:T(8,128)S(1)} %get-tuple-element.87), channel_id=1, source_target_pairs={{2,0},{0,2},{6,4},{4,6},{10,8},{8,10},{14,12},{12,14},{18,16},{16,... | collective-permute-start | bytes 1806344 | tf_op jit(solution)/shard_map/cond/branch_1_fun/ppermute | solution.py:376
  44.4 2.5 %collective-permute-start.8 = (f32[392,384]{1,0:T(8,128)S(1)}, f32[392,384]{1,0:T(8,128)S(1)}, u32[]{:S(2)}, u32[]{:S(2)}) collective-permute-start(f32[392,384]{1,0:T(8,128)S(1)} %get-tuple-element.89), channel_id=1, source_target_pairs={{2,0},{0,2},{6,4},{4,6},{10,8},{8,10},{14,12},{12,14},{18,16},{16,... | collective-permute-start | bytes 1806344 | tf_op jit(solution)/shard_map/cond/branch_1_fun/ppermute | solution.py:376
  47.5 6.3 %collective-permute-start.9 = (bf16[208,384]{1,0:T(8,128)(2,1)S(1)}, bf16[208,384]{1,0:T(8,128)(2,1)S(1)}, u32[]{:S(2)}, u32[]{:S(2)}) collective-permute-start(bf16[208,384]{1,0:T(8,128)(2,1)S(1)} %get-tuple-element.90), channel_id=1, source_target_pairs={{5,0},{4,1},{7,2},{6,3},{1,4},{0,5},{3,6},{2,7},{13,8},{12,9},{15,... | collective-permute-start | bytes 479240 | tf_op jit(solution)/shard_map/cond/branch_1_fun/ppermute | solution.py:405
  47.6 8.8 %collective-permute-start.10 = (bf16[208,384]{1,0:T(8,128)(2,1)S(1)}, bf16[208,384]{1,0:T(8,128)(2,1)S(1)}, u32[]{:S(2)}, u32[]{:S(2)}) collective-permute-start(bf16[208,384]{1,0:T(8,128)(2,1)S(1)} %get-tuple-element.91), channel_id=1, source_target_pairs={{0,1},{1,0},{2,3},{3,2},{4,5},{5,4},{6,7},{7,6},{8,9},{9,8},{10,11... | collective-permute-start | bytes 479240 | tf_op jit(solution)/shard_map/cond/branch_1_fun/ppermute | solution.py:407
  48.8 9.1 %collective-permute-start.11 = (bf16[208,384]{1,0:T(8,128)(2,1)S(1)}, bf16[208,384]{1,0:T(8,128)(2,1)S(1)}, u32[]{:S(2)}, u32[]{:S(2)}) collective-permute-start(bf16[208,384]{1,0:T(8,128)(2,1)S(1)} %get-tuple-element.92), channel_id=1, source_target_pairs={{4,0},{6,2},{0,4},{2,6},{12,8},{14,10},{8,12},{10,14},{20,16},{22,... | collective-permute-start | bytes 479240 | tf_op jit(solution)/shard_map/cond/branch_1_fun/ppermute | solution.py:376
  58.9 0.7 %copy-start.1 = (bf16[192,768]{1,0:T(8,128)(2,1)}, bf16[192,768]{1,0:T(8,128)(2,1)S(1)}, u32[]{:S(2)}) copy-start(bf16[192,768]{1,0:T(8,128)(2,1)S(1)} %get-tuple-element.143) | copy-start | bytes 884740

commit v2 on v1

--- a/solution.py
+++ b/solution.py
@@ -162,38 +162,47 @@
             jnp.where((first + j >= low) & (first + j < high), 0.0, -LOWEST).astype(jnp.float32)
             for j in range(count)
         ]
-        for h in range(heads):
-            own = head_columns(h)
-            scores = lax.dot_general(
-                jnp.concatenate([held[slot, tile_rows(2 * j), own] for j in range(count)], axis=0),
-                held_q[half, :, own],
+        maxima = [[state[half, pl.ds(columns + h, 1), tile_rows(t)] for t in range(tiles)] for h in range(heads)]
+        totals = [state[half, pl.ds(columns + heads + h, 1), :] for h in range(heads)]
+        scores = [
+            lax.dot_general(
+                jnp.concatenate([held[slot, tile_rows(2 * j), head_columns(h)] for j in range(count)], axis=0),
+                held_q[half, :, head_columns(h)],
                 (((1,), (1,)), ((), ())),
                 preferred_element_type=jnp.float32,
             )
-            max_at, total_at = pl.ds(columns + h, 1), pl.ds(columns + heads + h, 1)
-            factors, rounded, totals, maxima = [], [], [], []
+            for h in range(heads)
+        ]
+        factors, sums, updates, largest = [], [], [], []
+        for h in range(heads):
+            factor, rounded, total, new = [], [], [], []
             for t in range(tiles):
                 lanes = tile_rows(t)
-                parts = [scores[tile_rows(j), lanes] for j in range(count)]
-                old_max = state[half, max_at, lanes]
-                new_max = old_max
+                parts = [scores[h][tile_rows(j), lanes] for j in range(count)]
+                new_max = maxima[h][t]
                 for j in range(count):
                     new_max = jnp.maximum(new_max, jnp.max(parts[j], axis=0, keepdims=True) - off[j][:, lanes])
                 scaled = new_max * SCALE2
                 weights = [jnp.exp2(parts[j] * SCALE2 - (scaled + off[j][:, lanes])) for j in range(count)]
-                factors.append(jnp.exp2((old_max - new_max) * SCALE2))
-                totals.append(jnp.sum(functools.reduce(jnp.add, weights), axis=0, keepdims=True))
-                maxima.append(new_max)
+                factor.append(jnp.exp2((maxima[h][t] - new_max) * SCALE2))
+                total.append(jnp.sum(functools.reduce(jnp.add, weights), axis=0, keepdims=True))
+                new.append(new_max)
                 rounded.append(jnp.concatenate([w.astype(jnp.bfloat16) for w in weights], axis=0))
-            factor = jnp.concatenate(factors, axis=1)
-            update = jnp.dot(
-                jnp.concatenate([held[slot, tile_rows(2 * j + 1), own] for j in range(count)], axis=1),
-                jnp.concatenate(rounded, axis=1),
-                preferred_element_type=jnp.float32,
+            updates.append(
+                jnp.dot(
+                    jnp.concatenate([held[slot, tile_rows(2 * j + 1), head_columns(h)] for j in range(count)], axis=1),
+                    jnp.concatenate(rounded, axis=1),
+                    preferred_element_type=jnp.float32,
+                )
             )
-            state[half, own] = state[half, own] * factor + update
-            state[half, max_at] = jnp.concatenate(maxima, axis=1)
-            state[half, total_at] = state[half, total_at] * factor + jnp.concatenate(totals, axis=1)
+            factors.append(jnp.concatenate(factor, axis=1))
+            sums.append(jnp.concatenate(total, axis=1))
+            largest.append(jnp.concatenate(new, axis=1))
+        for h in range(heads):
+            own = head_columns(h)
+            state[half, own] = state[half, own] * factors[h] + updates[h]
+            state[half, pl.ds(columns + h, 1), :] = largest[h]
+            state[half, pl.ds(columns + heads + h, 1), :] = totals[h] * factors[h] + sums[h]
 
     @pl.loop(0, halves * len(places))
     def _(unit):
@@ -376,8 +385,10 @@
         return lax.ppermute(array, "seq", pairs)
 
     across = lambda s: s + 2 * flip(s)
-    along = lambda s: s + 4 * flip(s)
-    against = lambda s: s - 4 * flip(s)
+    near_side = lambda s: s + 4 * flip(s)
+    far_side = lambda s: s - 4 * flip(s)
+    along = lambda s: s + 4 * flip(s) * (1 - 2 * core(s))
+    against = lambda s: s - 4 * flip(s) * (1 - 2 * core(s))
     sibling = lambda s: s + 1 - 2 * core(s)
     inner = lambda s: core(s) == (1 - (s // 2) % 2)
 
@@ -411,7 +422,9 @@
         return merge([a1], [A1], states)
 
     def both_ways(block, a1, b1, states):
-        a2, b2 = moved(a1, along), moved(corner_of(b1, block), against, inner)
+        first = core(lax.axis_index("seq")) == 0
+        a2 = moved(jnp.where(first, a1, b1), near_side)
+        b2 = moved(corner_of(jnp.where(first, b1, a1), block), far_side, inner)
         states = fold([a1], [A1], states)
         return merge([a2, b2], [A2, B2], states, [None, lambda s: 2 * TILE * core(s)])
 

time: 59.9 us -> 41 us (0.68)
  the two profiles are of different devices: /device:TPU:9 before, /device:TPU:17 now
where the time goes in v2:
time: 41 us; the launch traced here: 40.8 us
  Pallas kernels  14.5 us (35%)
  starting transfers between devices  14.1 us (34%)
  waiting for transfers between devices  10.4 us (25%)
  between operations  0.76 us (2%)
  local copies, waits for them, and re-layouts  0.72 us (2%)
    pallas_call x5, Pallas kernels, attend(): pl.pallas_call(functools.partial(attend_kernel, which, places, arrays, no...  10.8 us
    ppermute x8, starting transfers between devices, moved(): return lax.ppermute(array, 'seq', pairs)  10.1 us
    ppermute x1, waiting for transfers between devices, merge(): over_both = lax.ppermute(over_both, ('seq', 'head'), pairs)  4.01 us
    ppermute x1, waiting for transfers between devices, merge(): over_x = lax.ppermute(over_x, 'head', [(0, 1), (1, 0)])  3.88 us
    ppermute x1, starting transfers between devices, merge(): over_both = lax.ppermute(over_both, ('seq', 'head'), pairs)  3.7 us
    ppermute x8, waiting for transfers between devices, moved(): return lax.ppermute(array, 'seq', pairs)  2.52 us
    pallas_call x1, Pallas kernels, pack(): pl.pallas_call(pack_kernel, out_shape=jax.ShapeDtypeStruct((2 * rows, col...  1.22 us
    pallas_call x1, Pallas kernels, meta(): pl.pallas_call(functools.partial(meta_kernel, halves), out_shape=[jax.Sha...  1.22 us
  transfers between devices with their start and end apart: 10, of which 4 were waited for; matrix products, arithmetic and copies ran while one was open for 0% of the time, Pallas kernels for 28%

profile of v2, /device:TPU:17, one launch (start us, length us, event | category | flops | bytes accessed | tf_op | source)
XLA Modules:
  0.0 40.8 jit_solution(6712079890686476545)
XLA Ops:
  0.0 0.0 copy-start.2
  0.0 0.0 copy-start
  0.0 1.2 %collective-permute-start.12 = (bf16[384,384]{1,0:T(8,128)(2,1)}, bf16[384,384]{1,0:T(8,128)(2,1)S(1)}, u32[]{:S(2)}, u32[]{:S(2)}) collective-permute-start(bf16[384,384]{1,0:T(8,128)(2,1)} %refs_0_.3), channel_id=1, source_target_pairs={{4,0},{6,2},{0,4},{2,6},{12,8},{14,10},{8,12},{10,14},{20,16},{22,... | collective-permute-start | bytes 884744 | tf_op jit(solution)/shard_map/ppermute | solution.py:385
  1.2 1.2 %pack.1.refs_2_ = bf16[768,384]{1,0:T(8,128)(2,1)S(1)} custom-call(bf16[384,384]{1,0:T(8,128)(2,1)} %k_ref.1, bf16[384,384]{1,0:T(8,128)(2,1)} %v_ref.1), custom_call_target="tpu_custom_call" | custom-call | tf_op jit(solution)/shard_map/pack/pallas_call | solution.py:99
  2.5 2.1 %collective-permute-start.16 = (bf16[768,384]{1,0:T(8,128)(2,1)S(1)}, bf16[768,384]{1,0:T(8,128)(2,1)S(1)}, u32[]{:S(2)}, u32[]{:S(2)}) collective-permute-start(bf16[768,384]{1,0:T(8,128)(2,1)S(1)} %pack.1.refs_2_), channel_id=1, source_target_pairs={{10,2},{12,4},{0,8},{18,10},{20,12},{6,14},{8,16},{26,18},{28,20},... | collective-permute-start | bytes 1769480 | tf_op jit(solution)/shard_map/ppermute | solution.py:385
  4.6 0.0 copy-done.2
  4.6 2.4 %collective-permute-start.14 = (bf16[384,384]{1,0:T(8,128)(2,1)S(1)}, bf16[384,384]{1,0:T(8,128)(2,1)S(1)}, u32[]{:S(2)}, u32[]{:S(2)}) collective-permute-start(bf16[384,384]{1,0:T(8,128)(2,1)S(1)} %copy-done.2), channel_id=1, source_target_pairs={{2,0},{0,2},{6,4},{4,6},{10,8},{8,10},{14,12},{12,14},{18,16},{16,... | collective-permute-start | bytes 884744 | tf_op jit(solution)/shard_map/ppermute | solution.py:385
  7.0 1.9 %collective-permute-start.13 = (bf16[768,384]{1,0:T(8,128)(2,1)S(1)}, bf16[768,384]{1,0:T(8,128)(2,1)S(1)}, u32[]{:S(2)}, u32[]{:S(2)}) collective-permute-start(bf16[768,384]{1,0:T(8,128)(2,1)S(1)} %pack.1.refs_2_), channel_id=1, source_target_pairs={{8,0},{14,6},{16,8},{2,10},{4,12},{22,14},{24,16},{10,18},{12,20},... | collective-permute-start | bytes 1769480 | tf_op jit(solution)/shard_map/ppermute | solution.py:385
  8.9 0.0 collective-permute-done.12.refs_0_.refs_2_
  8.9 0.7 %collective-permute-start.15 = (bf16[384,384]{1,0:T(8,128)(2,1)S(1)}, bf16[384,384]{1,0:T(8,128)(2,1)S(1)}, u32[]{:S(2)}, u32[]{:S(2)}) collective-permute-start(bf16[384,384]{1,0:T(8,128)(2,1)S(1)} %collective-permute-done.12.refs_0_.refs_2_), channel_id=1, source_target_pairs={{2,0},{0,2},{6,4},{4,6},{10,8},{8,10},{14,12},{12,14},{18,16},{16,... | collective-permute-start | bytes 884744 | tf_op jit(solution)/shard_map/ppermute | solution.py:385
  9.6 0.0 copy-done
  9.6 1.2 %meta.1 = (s32[8,384]{1,0:T(8,128)S(1)}, s32[1]{0:T(128)}) custom-call(s32[5]{0:T(128)S(1)} %copy-done), custom_call_target="tpu_custom_call" | custom-call | flops 536870912 | tf_op jit(solution)/shard_map/meta/pallas_call | solution.py:68
  11.5 0.0 collective-permute-done.14.refs_1_
  11.5 1.2 %attend.13 = (f32[392,384]{1,0:T(8,128)S(1)}, f32[392,384]{1,0:T(8,128)S(1)}) custom-call(s32[8,384]{1,0:T(8,128)S(1)} %get-tuple-element.105.bounds_ref, bf16[384,384]{1,0:T(8,128)(2,1)S(1)} %copy-done.2, bf16[384,384]{1,0:T(8,128)(2,1)S(1)} %collective-permute-done.14.refs_1_, bf16[768,384]{1,0:T(8,128)(2,1)S(1)} %pack.1.refs_2_), custom_call_target="tpu_custom_call" | custom-call | flops 905969664 | bytes 1769472 | tf_op jit(solution)/shard_map/attend/pallas_call | solution.py:230
  12.7 0.0 collective-permute-done.15.refs_1_.refs_3_
  12.7 2.0 %attend.14 = (f32[392,384]{1,0:T(8,128)S(1)}, f32[392,384]{1,0:T(8,128)S(1)}) custom-call(s32[8,384]{1,0:T(8,128)S(1)} %get-tuple-element.105.bounds_ref, bf16[384,384]{1,0:T(8,128)(2,1)S(1)} %collective-permute-done.12.refs_0_.refs_2_, bf16[384,384]{1,0:T(8,128)(2,1)S(1)} %collective-permute-done.15.refs_1_.refs_3_, bf16[768,384]{1,0:T(8,128)(2,1)S(1)} %pack.1.refs_2_), custom_call_target="tpu_custom_call" | custom-call | flops 905969664 | bytes 1769472 | tf_op jit(solution)/shard_map/attend/pallas_call | solution.py:230
  14.7 0.0 collective-permute-done.16.refs_4_
  14.7 4.4 %attend.15 = (f32[392,384]{1,0:T(8,128)}, f32[392,384]{1,0:T(8,128)}, f32[392,384]{1,0:T(8,128)}, f32[392,384]{1,0:T(8,128)}) custom-call(s32[8,384]{1,0:T(8,128)S(1)} %get-tuple-element.105.bounds_ref, bf16[384,384]{1,0:T(8,128)(2,1)S(1)} %copy-done.2, bf16[384,384]{1,0:T(8,128)(2,1)S(1)} %collective-permute-done.14.refs_1_, ...), custom_call_target="tpu_custom_call" | custom-call | flops 1811939328 | bytes 2949120 | tf_op jit(solution)/shard_map/attend/pallas_call | solution.py:230
  19.2 1.7 %collective-permute-done.13 = bf16[768,384]{1,0:T(8,128)(2,1)S(1)} collective-permute-done((bf16[768,384]{1,0:T(8,128)(2,1)S(1)}, bf16[768,384]{1,0:T(8,128)(2,1)S(1)}, u32[]{:S(2)}, u32[]{:S(2)}) %collective-permute-start.13) | collective-permute-done | bytes 589856 | tf_op jit(solution)/shard_map/ppermute | solution.py:385
  20.8 19.2 %conditional.1 = (bf16[192,768]{1,0:T(8,128)(2,1)S(1)}) conditional(s32[]{:T(128)} %bitcast, (s32[8,384]{1,0:T(8,128)S(1)}, bf16[384,384]{1,0:T(8,128)(2,1)S(1)}, bf16[384,384]{1,0:T(8,128)(2,1)S(1)}, bf16[768,384]{1,0:T(8,128)(2,1)S(1)}, f32[392,384]{1,0:T(8,128)}, /*index=5*/f32[392,384]{1,0:T(8,128)}, bf16[384,384]{1,0:T(8,128)(2,1)S(1)}, ...), branch_computations={%region_0.0_spmd, %region_1.2_spmd} | conditional | flops 5436407808 | bytes 20693432 | solution.py:431
  20.8 1.6 %attend.9 = (f32[392,384]{1,0:T(8,128)S(1)}, f32[392,384]{1,0:T(8,128)S(1)}) custom-call(s32[8,384]{1,0:T(8,128)S(1)} %get-tuple-element.52.bounds_ref, bf16[384,384]{1,0:T(8,128)(2,1)S(1)} %get-tuple-element.59.refs_0_, bf16[384,384]{1,0:T(8,128)(2,1)S(1)} %get-tuple-element.60.refs_1_, bf16[768,384]{1,0:T(8,128)(2,1)S(1)} %get-tuple-element.55.refs_2_, ...), custom_call_target="tpu_custom_call" | custom-call | flops 905969664 | bytes 1769472 | tf_op jit(solution)/shard_map/cond/branch_0_fun/attend/pallas_call | solution.py:230
  22.4 1.6 %collective-permute-start = (f32[392,384]{1,0:T(8,128)S(1)}, f32[392,384]{1,0:T(8,128)S(1)}, u32[]{:S(2)}, u32[]{:S(2)}) collective-permute-start(f32[392,384]{1,0:T(8,128)S(1)} %get-tuple-element.63), channel_id=1, source_target_pairs={{2,0},{0,2},{6,4},{4,6},{10,8},{8,10},{14,12},{12,14},{18,16},{16,... | collective-permute-start | bytes 1806344 | tf_op jit(solution)/shard_map/cond/branch_0_fun/ppermute | solution.py:385
  24.0 0.1 collective-permute-start.1
  24.1 1.6 %attend.8 = (f32[392,384]{1,0:T(8,128)S(1)}, f32[392,384]{1,0:T(8,128)S(1)}) custom-call(s32[8,384]{1,0:T(8,128)S(1)} %get-tuple-element.52.bounds_ref, bf16[384,384]{1,0:T(8,128)(2,1)S(1)} %get-tuple-element.53.refs_0_, bf16[384,384]{1,0:T(8,128)(2,1)S(1)} %get-tuple-element.54.refs_1_, bf16[768,384]{1,0:T(8,128)(2,1)S(1)} %get-tuple-element.55.refs_2_, ...), custom_call_target="tpu_custom_call" | custom-call | flops 905969664 | bytes 1769472 | tf_op jit(solution)/shard_map/cond/branch_0_fun/attend/pallas_call | solution.py:230
  25.7 0.0 collective-permute-done.refs_1_
  25.7 0.8 %collective-permute-done.1.refs_3_ = f32[392,384]{1,0:T(8,128)S(1)} collective-permute-done((f32[392,384]{1,0:T(8,128)S(1)}, f32[392,384]{1,0:T(8,128)S(1)}, u32[]{:S(2)}, u32[]{:S(2)}) %collective-permute-start.1) | collective-permute-done | bytes 602144 | tf_op jit(solution)/shard_map/cond/branch_0_fun/ppermute | solution.py:385
  26.5 0.5 %message.2 = (bf16[208,384]{1,0:T(8,128)(2,1)S(1)}, bf16[208,384]{1,0:T(8,128)(2,1)S(1)}, bf16[208,384]{1,0:T(8,128)(2,1)S(1)}, bf16[208,384]{1,0:T(8,128)(2,1)S(1)}) custom-call(f32[392,384]{1,0:T(8,128)S(1)} %get-tuple-element.58.refs_0_, f32[392,384]{1,0:T(8,128)S(1)} %collective-permute-done.refs_1_, f32[392,384]{1,0:T(8,128)S(1)} %get-tuple-element.64.refs_2_, ...), custom_call_target="tpu_custom_call" | custom-call | tf_op jit(solution)/shard_map/cond/branch_0_fun/message/pallas_call | solution.py:313
  27.0 3.7 %collective-permute-start.2 = (bf16[208,384]{1,0:T(8,128)(2,1)S(1)}, bf16[208,384]{1,0:T(8,128)(2,1)S(1)}, u32[]{:S(2)}, u32[]{:S(2)}) collective-permute-start(bf16[208,384]{1,0:T(8,128)(2,1)S(1)} %get-tuple-element.66), channel_id=1, source_target_pairs={{5,0},{4,1},{7,2},{6,3},{1,4},{0,5},{3,6},{2,7},{13,8},{12,9},{15,... | collective-permute-start | bytes 479240 | tf_op jit(solution)/shard_map/cond/branch_0_fun/ppermute | solution.py:416
  30.7 0.3 collective-permute-start.3
  31.0 0.1 collective-permute-start.4
  31.1 4.0 %collective-permute-done.2.refs_0_ = bf16[208,384]{1,0:T(8,128)(2,1)S(1)} collective-permute-done((bf16[208,384]{1,0:T(8,128)(2,1)S(1)}, bf16[208,384]{1,0:T(8,128)(2,1)S(1)}, u32[]{:S(2)}, u32[]{:S(2)}) %collective-permute-start.2) | collective-permute-done | bytes 159776 | tf_op jit(solution)/shard_map/cond/branch_0_fun/ppermute | solution.py:416
  35.1 3.9 %collective-permute-done.3.refs_1_ = bf16[208,384]{1,0:T(8,128)(2,1)S(1)} collective-permute-done((bf16[208,384]{1,0:T(8,128)(2,1)S(1)}, bf16[208,384]{1,0:T(8,128)(2,1)S(1)}, u32[]{:S(2)}, u32[]{:S(2)}) %collective-permute-start.3) | collective-permute-done | bytes 159776 | tf_op jit(solution)/shard_map/cond/branch_0_fun/ppermute | solution.py:418
  39.0 0.0 collective-permute-done.4.refs_2_
  39.0 0.8 %settle.2 = bf16[192,768]{1,0:T(8,128)(2,1)S(1)} custom-call(bf16[208,384]{1,0:T(8,128)(2,1)S(1)} %collective-permute-done.2.refs_0_, bf16[208,384]{1,0:T(8,128)(2,1)S(1)} %collective-permute-done.3.refs_1_, bf16[208,384]{1,0:T(8,128)(2,1)S(1)} %collective-permute-done.4.refs_2_, bf16[208,384]{1,0:T(8,128)(2,1)S(1)} %get-tuple-element.69.refs_3_), custom_call_target="tpu_custom_call" | custom-call | tf_op jit(solution)/shard_map/cond/branch_0_fun/settle/pallas_call | solution.py:350
  40.0 0.0 copy-start.1
  40.1 0.7 %copy-done.1 = bf16[192,768]{1,0:T(8,128)(2,1)} copy-done((bf16[192,768]{1,0:T(8,128)(2,1)}, bf16[192,768]{1,0:T(8,128)(2,1)S(1)}, u32[]{:S(2)}) %copy-start.1) | copy-done | bytes 294936
Async XLA Ops:
  0.0 4.6 %copy-start.2 = (bf16[384,384]{1,0:T(8,128)(2,1)S(1)}, bf16[384,384]{1,0:T(8,128)(2,1)}, u32[]{:S(2)}) copy-start(bf16[384,384]{1,0:T(8,128)(2,1)} %refs_0_.3) | copy-start | bytes 884740
  0.0 9.6 %copy-start = (s32[5]{0:T(128)S(1)}, s32[5]{0:T(128)}, u32[]{:S(2)}) copy-start(s32[5]{0:T(128)} %tiles_ref.1) | copy-start | bytes 64
  0.0 8.9 %collective-permute-start.12 = (bf16[384,384]{1,0:T(8,128)(2,1)}, bf16[384,384]{1,0:T(8,128)(2,1)S(1)}, u32[]{:S(2)}, u32[]{:S(2)}) collective-permute-start(bf16[384,384]{1,0:T(8,128)(2,1)} %refs_0_.3), channel_id=1, source_target_pairs={{4,0},{6,2},{0,4},{2,6},{12,8},{14,10},{8,12},{10,14},{20,16},{22,... | collective-permute-start | bytes 884744 | tf_op jit(solution)/shard_map/ppermute | solution.py:385
  2.5 12.2 %collective-permute-start.16 = (bf16[768,384]{1,0:T(8,128)(2,1)S(1)}, bf16[768,384]{1,0:T(8,128)(2,1)S(1)}, u32[]{:S(2)}, u32[]{:S(2)}) collective-permute-start(bf16[768,384]{1,0:T(8,128)(2,1)S(1)} %pack.1.refs_2_), channel_id=1, source_target_pairs={{10,2},{12,4},{0,8},{18,10},{20,12},{6,14},{8,16},{26,18},{28,20},... | collective-permute-start | bytes 1769480 | tf_op jit(solution)/shard_map/ppermute | solution.py:385
  4.6 6.9 %collective-permute-start.14 = (bf16[384,384]{1,0:T(8,128)(2,1)S(1)}, bf16[384,384]{1,0:T(8,128)(2,1)S(1)}, u32[]{:S(2)}, u32[]{:S(2)}) collective-permute-start(bf16[384,384]{1,0:T(8,128)(2,1)S(1)} %copy-done.2), channel_id=1, source_target_pairs={{2,0},{0,2},{6,4},{4,6},{10,8},{8,10},{14,12},{12,14},{18,16},{16,... | collective-permute-start | bytes 884744 | tf_op jit(solution)/shard_map/ppermute | solution.py:385
  7.0 13.8 %collective-permute-start.13 = (bf16[768,384]{1,0:T(8,128)(2,1)S(1)}, bf16[768,384]{1,0:T(8,128)(2,1)S(1)}, u32[]{:S(2)}, u32[]{:S(2)}) collective-permute-start(bf16[768,384]{1,0:T(8,128)(2,1)S(1)} %pack.1.refs_2_), channel_id=1, source_target_pairs={{8,0},{14,6},{16,8},{2,10},{4,12},{22,14},{24,16},{10,18},{12,20},... | collective-permute-start | bytes 1769480 | tf_op jit(solution)/shard_map/ppermute | solution.py:385
  8.9 3.8 %collective-permute-start.15 = (bf16[384,384]{1,0:T(8,128)(2,1)S(1)}, bf16[384,384]{1,0:T(8,128)(2,1)S(1)}, u32[]{:S(2)}, u32[]{:S(2)}) collective-permute-start(bf16[384,384]{1,0:T(8,128)(2,1)S(1)} %collective-permute-done.12.refs_0_.refs_2_), channel_id=1, source_target_pairs={{2,0},{0,2},{6,4},{4,6},{10,8},{8,10},{14,12},{12,14},{18,16},{16,... | collective-permute-start | bytes 884744 | tf_op jit(solution)/shard_map/ppermute | solution.py:385
  22.4 3.2 %collective-permute-start = (f32[392,384]{1,0:T(8,128)S(1)}, f32[392,384]{1,0:T(8,128)S(1)}, u32[]{:S(2)}, u32[]{:S(2)}) collective-permute-start(f32[392,384]{1,0:T(8,128)S(1)} %get-tuple-element.63), channel_id=1, source_target_pairs={{2,0},{0,2},{6,4},{4,6},{10,8},{8,10},{14,12},{12,14},{18,16},{16,... | collective-permute-start | bytes 1806344 | tf_op jit(solution)/shard_map/cond/branch_0_fun/ppermute | solution.py:385
  24.0 2.5 %collective-permute-start.1 = (f32[392,384]{1,0:T(8,128)S(1)}, f32[392,384]{1,0:T(8,128)S(1)}, u32[]{:S(2)}, u32[]{:S(2)}) collective-permute-start(f32[392,384]{1,0:T(8,128)S(1)} %get-tuple-element.65), channel_id=1, source_target_pairs={{2,0},{0,2},{6,4},{4,6},{10,8},{8,10},{14,12},{12,14},{18,16},{16,... | collective-permute-start | bytes 1806344 | tf_op jit(solution)/shard_map/cond/branch_0_fun/ppermute | solution.py:385
  27.0 8.1 %collective-permute-start.2 = (bf16[208,384]{1,0:T(8,128)(2,1)S(1)}, bf16[208,384]{1,0:T(8,128)(2,1)S(1)}, u32[]{:S(2)}, u32[]{:S(2)}) collective-permute-start(bf16[208,384]{1,0:T(8,128)(2,1)S(1)} %get-tuple-element.66), channel_id=1, source_target_pairs={{5,0},{4,1},{7,2},{6,3},{1,4},{0,5},{3,6},{2,7},{13,8},{12,9},{15,... | collective-permute-start | bytes 479240 | tf_op jit(solution)/shard_map/cond/branch_0_fun/ppermute | solution.py:416
  30.7 8.3 %collective-permute-start.3 = (bf16[208,384]{1,0:T(8,128)(2,1)S(1)}, bf16[208,384]{1,0:T(8,128)(2,1)S(1)}, u32[]{:S(2)}, u32[]{:S(2)}) collective-permute-start(bf16[208,384]{1,0:T(8,128)(2,1)S(1)} %get-tuple-element.67), channel_id=1, source_target_pairs={{0,1},{1,0},{2,3},{3,2},{4,5},{5,4},{6,7},{7,6},{8,9},{9,8},{10,11... | collective-permute-start | bytes 479240 | tf_op jit(solution)/shard_map/cond/branch_0_fun/ppermute | solution.py:418
  31.0 8.0 %collective-permute-start.4 = (bf16[208,384]{1,0:T(8,128)(2,1)S(1)}, bf16[208,384]{1,0:T(8,128)(2,1)S(1)}, u32[]{:S(2)}, u32[]{:S(2)}) collective-permute-start(bf16[208,384]{1,0:T(8,128)(2,1)S(1)} %get-tuple-element.68), channel_id=1, source_target_pairs={{4,0},{6,2},{0,4},{2,6},{12,8},{14,10},{8,12},{10,14},{20,16},{22,... | collective-permute-start | bytes 479240 | tf_op jit(solution)/shard_map/cond/branch_0_fun/ppermute | solution.py:385
  40.0 0.7 %copy-start.1 = (bf16[192,768]{1,0:T(8,128)(2,1)}, bf16[192,768]{1,0:T(8,128)(2,1)S(1)}, u32[]{:S(2)}) copy-start(bf16[192,768]{1,0:T(8,128)(2,1)S(1)} %get-tuple-element.147) | copy-start | bytes 884740

commit v3 on v2

--- a/solution.py
+++ b/solution.py
@@ -22,7 +22,7 @@
 
 
 def params():
-    return pltpu.CompilerParams(vmem_limit_bytes=24 * 1024 * 1024)
+    return pltpu.CompilerParams(vmem_limit_bytes=16 * 1024 * 1024)
 
 
 def head_columns(h):

time: 41 us -> 56 us (1.37)
  the two profiles are of different devices: /device:TPU:17 before, /device:TPU:0 now
where the time goes in v3:
time: 56 us; the launch traced here: 55.9 us
  waiting for transfers between devices  23 us (41%)
  starting transfers between devices  15.6 us (28%)
  Pallas kernels  15.4 us (28%)
  between operations  0.75 us (1%)
  local copies, waits for them, and re-layouts  0.72 us (1%)
    ppermute x10, waiting for transfers between devices, moved(): return lax.ppermute(array, 'seq', pairs)  16.8 us
    ppermute x10, starting transfers between devices, moved(): return lax.ppermute(array, 'seq', pairs)  13.5 us
    pallas_call x6, Pallas kernels, attend(): pl.pallas_call(functools.partial(attend_kernel, which, places, arrays, no...  11.6 us
    ppermute x1, waiting for transfers between devices, merge(): over_both = lax.ppermute(over_both, ('seq', 'head'), pairs)  4.38 us
    ppermute x1, waiting for transfers between devices, merge(): over_x = lax.ppermute(over_x, 'head', [(0, 1), (1, 0)])  1.75 us
    ppermute x1, starting transfers between devices, merge(): over_both = lax.ppermute(over_both, ('seq', 'head'), pairs)  1.58 us
    pallas_call x1, Pallas kernels, pack(): pl.pallas_call(pack_kernel, out_shape=jax.ShapeDtypeStruct((2 * rows, col...  1.22 us
    pallas_call x1, Pallas kernels, meta(): pl.pallas_call(functools.partial(meta_kernel, halves), out_shape=[jax.Sha...  1.22 us
  transfers between devices with their start and end apart: 12, of which 9 were waited for; matrix products, arithmetic and copies ran while one was open for 0% of the time, Pallas kernels for 23%

profile of v3, /device:TPU:0, one launch (start us, length us, event | category | flops | bytes accessed | tf_op | source)
XLA Modules:
  0.0 55.9 jit_solution(14678809951435130961)
XLA Ops:
  0.0 0.0 copy-start.2
  0.0 0.0 copy-start
  0.0 3.0 %collective-permute-start.12 = (bf16[384,384]{1,0:T(8,128)(2,1)}, bf16[384,384]{1,0:T(8,128)(2,1)S(1)}, u32[]{:S(2)}, u32[]{:S(2)}) collective-permute-start(bf16[384,384]{1,0:T(8,128)(2,1)} %refs_0_.3), channel_id=1, source_target_pairs={{4,0},{6,2},{0,4},{2,6},{12,8},{14,10},{8,12},{10,14},{20,16},{22,... | collective-permute-start | bytes 884744 | tf_op jit(solution)/shard_map/ppermute | solution.py:385
  3.0 1.2 %pack.1.refs_2_ = bf16[768,384]{1,0:T(8,128)(2,1)S(1)} custom-call(bf16[384,384]{1,0:T(8,128)(2,1)} %k_ref.1, bf16[384,384]{1,0:T(8,128)(2,1)} %v_ref.1), custom_call_target="tpu_custom_call" | custom-call | tf_op jit(solution)/shard_map/pack/pallas_call | solution.py:99
  4.2 3.5 %collective-permute-start.16 = (bf16[768,384]{1,0:T(8,128)(2,1)S(1)}, bf16[768,384]{1,0:T(8,128)(2,1)S(1)}, u32[]{:S(2)}, u32[]{:S(2)}) collective-permute-start(bf16[768,384]{1,0:T(8,128)(2,1)S(1)} %pack.1.refs_2_), channel_id=1, source_target_pairs={{10,2},{12,4},{0,8},{18,10},{20,12},{6,14},{8,16},{26,18},{28,20},... | collective-permute-start | bytes 1769480 | tf_op jit(solution)/shard_map/ppermute | solution.py:385
  7.7 0.0 copy-done.2
  7.7 0.1 collective-permute-start.14
  7.8 1.3 %collective-permute-start.13 = (bf16[768,384]{1,0:T(8,128)(2,1)S(1)}, bf16[768,384]{1,0:T(8,128)(2,1)S(1)}, u32[]{:S(2)}, u32[]{:S(2)}) collective-permute-start(bf16[768,384]{1,0:T(8,128)(2,1)S(1)} %pack.1.refs_2_), channel_id=1, source_target_pairs={{8,0},{14,6},{16,8},{2,10},{4,12},{22,14},{24,16},{10,18},{12,20},... | collective-permute-start | bytes 1769480 | tf_op jit(solution)/shard_map/ppermute | solution.py:385
  9.1 1.1 %collective-permute-done.12.refs_0_.refs_2_ = bf16[384,384]{1,0:T(8,128)(2,1)S(1)} collective-permute-done((bf16[384,384]{1,0:T(8,128)(2,1)}, bf16[384,384]{1,0:T(8,128)(2,1)S(1)}, u32[]{:S(2)}, u32[]{:S(2)}) %collective-permute-start.12) | collective-permute-done | bytes 294944 | tf_op jit(solution)/shard_map/ppermute | solution.py:385
  10.3 1.3 %collective-permute-start.15 = (bf16[384,384]{1,0:T(8,128)(2,1)S(1)}, bf16[384,384]{1,0:T(8,128)(2,1)S(1)}, u32[]{:S(2)}, u32[]{:S(2)}) collective-permute-start(bf16[384,384]{1,0:T(8,128)(2,1)S(1)} %collective-permute-done.12.refs_0_.refs_2_), channel_id=1, source_target_pairs={{2,0},{0,2},{6,4},{4,6},{10,8},{8,10},{14,12},{12,14},{18,16},{16,... | collective-permute-start | bytes 884744 | tf_op jit(solution)/shard_map/ppermute | solution.py:385
  11.6 0.0 copy-done
  11.6 1.2 %meta.1 = (s32[8,384]{1,0:T(8,128)S(1)}, s32[1]{0:T(128)}) custom-call(s32[5]{0:T(128)S(1)} %copy-done), custom_call_target="tpu_custom_call" | custom-call | flops 536870912 | tf_op jit(solution)/shard_map/meta/pallas_call | solution.py:68
  13.5 0.0 collective-permute-done.14.refs_1_
  13.5 2.0 %attend.13 = (f32[392,384]{1,0:T(8,128)S(1)}, f32[392,384]{1,0:T(8,128)S(1)}) custom-call(s32[8,384]{1,0:T(8,128)S(1)} %get-tuple-element.105.bounds_ref, bf16[384,384]{1,0:T(8,128)(2,1)S(1)} %copy-done.2, bf16[384,384]{1,0:T(8,128)(2,1)S(1)} %collective-permute-done.14.refs_1_, bf16[768,384]{1,0:T(8,128)(2,1)S(1)} %pack.1.refs_2_), custom_call_target="tpu_custom_call" | custom-call | flops 905969664 | bytes 1769472 | tf_op jit(solution)/shard_map/attend/pallas_call | solution.py:230
  15.5 0.0 collective-permute-done.15.refs_1_.refs_3_
  15.5 1.2 %attend.14 = (f32[392,384]{1,0:T(8,128)S(1)}, f32[392,384]{1,0:T(8,128)S(1)}) custom-call(s32[8,384]{1,0:T(8,128)S(1)} %get-tuple-element.105.bounds_ref, bf16[384,384]{1,0:T(8,128)(2,1)S(1)} %collective-permute-done.12.refs_0_.refs_2_, bf16[384,384]{1,0:T(8,128)(2,1)S(1)} %collective-permute-done.15.refs_1_.refs_3_, bf16[768,384]{1,0:T(8,128)(2,1)S(1)} %pack.1.refs_2_), custom_call_target="tpu_custom_call" | custom-call | flops 905969664 | bytes 1769472 | tf_op jit(solution)/shard_map/attend/pallas_call | solution.py:230
  16.7 1.6 %collective-permute-done.16.refs_4_ = bf16[768,384]{1,0:T(8,128)(2,1)S(1)} collective-permute-done((bf16[768,384]{1,0:T(8,128)(2,1)S(1)}, bf16[768,384]{1,0:T(8,128)(2,1)S(1)}, u32[]{:S(2)}, u32[]{:S(2)}) %collective-permute-start.16) | collective-permute-done | bytes 589856 | tf_op jit(solution)/shard_map/ppermute | solution.py:385
  18.2 1.9 %attend.15 = (f32[392,384]{1,0:T(8,128)}, f32[392,384]{1,0:T(8,128)}, f32[392,384]{1,0:T(8,128)}, f32[392,384]{1,0:T(8,128)}) custom-call(s32[8,384]{1,0:T(8,128)S(1)} %get-tuple-element.105.bounds_ref, bf16[384,384]{1,0:T(8,128)(2,1)S(1)} %copy-done.2, bf16[384,384]{1,0:T(8,128)(2,1)S(1)} %collective-permute-done.14.refs_1_, ...), custom_call_target="tpu_custom_call" | custom-call | flops 1811939328 | bytes 2949120 | tf_op jit(solution)/shard_map/attend/pallas_call | solution.py:230
  20.1 0.8 %collective-permute-done.13 = bf16[768,384]{1,0:T(8,128)(2,1)S(1)} collective-permute-done((bf16[768,384]{1,0:T(8,128)(2,1)S(1)}, bf16[768,384]{1,0:T(8,128)(2,1)S(1)}, u32[]{:S(2)}, u32[]{:S(2)}) %collective-permute-start.13) | collective-permute-done | bytes 589856 | tf_op jit(solution)/shard_map/ppermute | solution.py:385
  20.9 34.3 %conditional.1 = (bf16[192,768]{1,0:T(8,128)(2,1)S(1)}) conditional(s32[]{:T(128)} %bitcast, (s32[8,384]{1,0:T(8,128)S(1)}, bf16[384,384]{1,0:T(8,128)(2,1)S(1)}, bf16[384,384]{1,0:T(8,128)(2,1)S(1)}, bf16[768,384]{1,0:T(8,128)(2,1)S(1)}, f32[392,384]{1,0:T(8,128)}, /*index=5*/f32[392,384]{1,0:T(8,128)}, bf16[384,384]{1,0:T(8,128)(2,1)S(1)}, ...), branch_computations={%region_0.0_spmd, %region_1.2_spmd} | conditional | flops 5436407808 | bytes 20693432 | solution.py:431
  20.9 0.1 broadcast_select_fusion
  21.0 1.3 %collective-permute-start.5 = (bf16[768,384]{1,0:T(8,128)(2,1)S(1)}, bf16[768,384]{1,0:T(8,128)(2,1)S(1)}, u32[]{:S(2)}, u32[]{:S(2)}) collective-permute-start(bf16[768,384]{1,0:T(8,128)(2,1)S(1)} %get-tuple-element.116), channel_id=1, source_target_pairs={{8,0},{10,2},{16,8},{18,10},{4,12},{6,14},{24,16},{26,18},{12,20},... | collective-permute-start | bytes 1769480 | tf_op jit(solution)/shard_map/cond/branch_1_fun/ppermute | solution.py:385
  22.3 0.1 corner.1
  22.4 0.9 %collective-permute-start.6 = (bf16[512,384]{1,0:T(8,128)(2,1)S(1)}, bf16[512,384]{1,0:T(8,128)(2,1)S(1)}, u32[]{:S(2)}, u32[]{:S(2)}) collective-permute-start(bf16[512,384]{1,0:T(8,128)(2,1)S(1)} %corner.1), channel_id=1, source_target_pairs={{12,4},{2,10},{20,12},{10,18},{28,20},{18,26},{13,5},{3,11},{21,13... | collective-permute-start | bytes 1179656 | tf_op jit(solution)/shard_map/cond/branch_1_fun/ppermute | solution.py:385
  23.2 3.9 %attend.10 = (f32[392,384]{1,0:T(8,128)S(1)}, f32[392,384]{1,0:T(8,128)S(1)}, f32[392,384]{1,0:T(8,128)S(1)}, f32[392,384]{1,0:T(8,128)S(1)}) custom-call(s32[8,384]{1,0:T(8,128)S(1)} %get-tuple-element.70.bounds_ref, bf16[384,384]{1,0:T(8,128)(2,1)S(1)} %get-tuple-element.71.refs_0_, bf16[384,384]{1,0:T(8,128)(2,1)S(1)} %get-tuple-element.76.refs_1_.refs_0_, ...), custom_call_target="tpu_custom_call" | custom-call | flops 1811939328 | bytes 2949120 | tf_op jit(solution)/shard_map/cond/branch_1_fun/attend/pallas_call | solution.py:230
  27.2 0.0 collective-permute-done.6.refs_3_
  27.2 11.2 %collective-permute-done.5.refs_2_ = bf16[768,384]{1,0:T(8,128)(2,1)S(1)} collective-permute-done((bf16[768,384]{1,0:T(8,128)(2,1)S(1)}, bf16[768,384]{1,0:T(8,128)(2,1)S(1)}, u32[]{:S(2)}, u32[]{:S(2)}) %collective-permute-start.5) | collective-permute-done | bytes 589856 | tf_op jit(solution)/shard_map/cond/branch_1_fun/ppermute | solution.py:385
  38.4 1.3 %attend.12 = (f32[392,384]{1,0:T(8,128)S(1)}, f32[392,384]{1,0:T(8,128)S(1)}) custom-call(s32[8,384]{1,0:T(8,128)S(1)} %get-tuple-element.70.bounds_ref, bf16[384,384]{1,0:T(8,128)(2,1)S(1)} %get-tuple-element.76.refs_1_.refs_0_, bf16[384,384]{1,0:T(8,128)(2,1)S(1)} %get-tuple-element.77.refs_3_.refs_1_, ...), custom_call_target="tpu_custom_call" | custom-call | flops 1811939328 | bytes 2359296 | tf_op jit(solution)/shard_map/cond/branch_1_fun/attend/pallas_call | solution.py:230
  39.7 0.6 %collective-permute-start.7 = (f32[392,384]{1,0:T(8,128)S(1)}, f32[392,384]{1,0:T(8,128)S(1)}, u32[]{:S(2)}, u32[]{:S(2)}) collective-permute-start(f32[392,384]{1,0:T(8,128)S(1)} %get-tuple-element.87), channel_id=1, source_target_pairs={{2,0},{0,2},{6,4},{4,6},{10,8},{8,10},{14,12},{12,14},{18,16},{16,... | collective-permute-start | bytes 1806344 | tf_op jit(solution)/shard_map/cond/branch_1_fun/ppermute | solution.py:385
  40.3 0.1 collective-permute-start.8
  40.4 1.3 %attend.11 = (f32[392,384]{1,0:T(8,128)S(1)}, f32[392,384]{1,0:T(8,128)S(1)}) custom-call(s32[8,384]{1,0:T(8,128)S(1)} %get-tuple-element.70.bounds_ref, bf16[384,384]{1,0:T(8,128)(2,1)S(1)} %get-tuple-element.71.refs_0_, bf16[384,384]{1,0:T(8,128)(2,1)S(1)} %get-tuple-element.72.refs_2_.refs_1_, bf16[768,384]{1,0:T(8,128)(2,1)S(1)} %collective-permute-done.5.refs_2_, ...), custom_call_target="tpu_custom_call" | custom-call | flops 1811939328 | bytes 2359296 | tf_op jit(solution)/shard_map/cond/branch_1_fun/attend/pallas_call | solution.py:230
  41.7 0.2 collective-permute-done.7.refs_1_
  42.0 0.9 %collective-permute-done.8.refs_3_ = f32[392,384]{1,0:T(8,128)S(1)} collective-permute-done((f32[392,384]{1,0:T(8,128)S(1)}, f32[392,384]{1,0:T(8,128)S(1)}, u32[]{:S(2)}, u32[]{:S(2)}) %collective-permute-start.8) | collective-permute-done | bytes 602144 | tf_op jit(solution)/shard_map/cond/branch_1_fun/ppermute | solution.py:385
  42.8 0.5 message.3
  43.4 1.6 %collective-permute-start.9 = (bf16[208,384]{1,0:T(8,128)(2,1)S(1)}, bf16[208,384]{1,0:T(8,128)(2,1)S(1)}, u32[]{:S(2)}, u32[]{:S(2)}) collective-permute-start(bf16[208,384]{1,0:T(8,128)(2,1)S(1)} %get-tuple-element.90), channel_id=1, source_target_pairs={{5,0},{4,1},{7,2},{6,3},{1,4},{0,5},{3,6},{2,7},{13,8},{12,9},{15,... | collective-permute-start | bytes 479240 | tf_op jit(solution)/shard_map/cond/branch_1_fun/ppermute | solution.py:416
  44.9 0.6 %collective-permute-start.10 = (bf16[208,384]{1,0:T(8,128)(2,1)S(1)}, bf16[208,384]{1,0:T(8,128)(2,1)S(1)}, u32[]{:S(2)}, u32[]{:S(2)}) collective-permute-start(bf16[208,384]{1,0:T(8,128)(2,1)S(1)} %get-tuple-element.91), channel_id=1, source_target_pairs={{0,1},{1,0},{2,3},{3,2},{4,5},{5,4},{6,7},{7,6},{8,9},{9,8},{10,11... | collective-permute-start | bytes 479240 | tf_op jit(solution)/shard_map/cond/branch_1_fun/ppermute | solution.py:418
  45.5 1.4 %collective-permute-start.11 = (bf16[208,384]{1,0:T(8,128)(2,1)S(1)}, bf16[208,384]{1,0:T(8,128)(2,1)S(1)}, u32[]{:S(2)}, u32[]{:S(2)}) collective-permute-start(bf16[208,384]{1,0:T(8,128)(2,1)S(1)} %get-tuple-element.92), channel_id=1, source_target_pairs={{4,0},{6,2},{0,4},{2,6},{12,8},{14,10},{8,12},{10,14},{20,16},{22,... | collective-permute-start | bytes 479240 | tf_op jit(solution)/shard_map/cond/branch_1_fun/ppermute | solution.py:385
  46.9 4.4 %collective-permute-done.9.refs_0_ = bf16[208,384]{1,0:T(8,128)(2,1)S(1)} collective-permute-done((bf16[208,384]{1,0:T(8,128)(2,1)S(1)}, bf16[208,384]{1,0:T(8,128)(2,1)S(1)}, u32[]{:S(2)}, u32[]{:S(2)}) %collective-permute-start.9) | collective-permute-done | bytes 159776 | tf_op jit(solution)/shard_map/cond/branch_1_fun/ppermute | solution.py:416
  51.3 1.7 %collective-permute-done.10.refs_1_ = bf16[208,384]{1,0:T(8,128)(2,1)S(1)} collective-permute-done((bf16[208,384]{1,0:T(8,128)(2,1)S(1)}, bf16[208,384]{1,0:T(8,128)(2,1)S(1)}, u32[]{:S(2)}, u32[]{:S(2)}) %collective-permute-start.10) | collective-permute-done | bytes 159776 | tf_op jit(solution)/shard_map/cond/branch_1_fun/ppermute | solution.py:418
  53.1 1.1 %collective-permute-done.11.refs_2_ = bf16[208,384]{1,0:T(8,128)(2,1)S(1)} collective-permute-done((bf16[208,384]{1,0:T(8,128)(2,1)S(1)}, bf16[208,384]{1,0:T(8,128)(2,1)S(1)}, u32[]{:S(2)}, u32[]{:S(2)}) %collective-permute-start.11) | collective-permute-done | bytes 159776 | tf_op jit(solution)/shard_map/cond/branch_1_fun/ppermute | solution.py:385
  54.1 0.8 %settle.3 = bf16[192,768]{1,0:T(8,128)(2,1)S(1)} custom-call(bf16[208,384]{1,0:T(8,128)(2,1)S(1)} %collective-permute-done.9.refs_0_, bf16[208,384]{1,0:T(8,128)(2,1)S(1)} %collective-permute-done.10.refs_1_, bf16[208,384]{1,0:T(8,128)(2,1)S(1)} %collective-permute-done.11.refs_2_, bf16[208,384]{1,0:T(8,128)(2,1)S(1)} %get-tuple-element.93.refs_3_), custom_call_target="tpu_custom_call" | custom-call | tf_op jit(solution)/shard_map/cond/branch_1_fun/settle/pallas_call | solution.py:350
  55.2 0.0 copy-start.1
  55.2 0.7 %copy-done.1 = bf16[192,768]{1,0:T(8,128)(2,1)} copy-done((bf16[192,768]{1,0:T(8,128)(2,1)}, bf16[192,768]{1,0:T(8,128)(2,1)S(1)}, u32[]{:S(2)}) %copy-start.1) | copy-done | bytes 294936
Async XLA Ops:
  0.0 7.7 %copy-start.2 = (bf16[384,384]{1,0:T(8,128)(2,1)S(1)}, bf16[384,384]{1,0:T(8,128)(2,1)}, u32[]{:S(2)}) copy-start(bf16[384,384]{1,0:T(8,128)(2,1)} %refs_0_.3) | copy-start | bytes 884740
  0.0 11.6 %copy-start = (s32[5]{0:T(128)S(1)}, s32[5]{0:T(128)}, u32[]{:S(2)}) copy-start(s32[5]{0:T(128)} %tiles_ref.1) | copy-start | bytes 64
  0.0 10.3 %collective-permute-start.12 = (bf16[384,384]{1,0:T(8,128)(2,1)}, bf16[384,384]{1,0:T(8,128)(2,1)S(1)}, u32[]{:S(2)}, u32[]{:S(2)}) collective-permute-start(bf16[384,384]{1,0:T(8,128)(2,1)} %refs_0_.3), channel_id=1, source_target_pairs={{4,0},{6,2},{0,4},{2,6},{12,8},{14,10},{8,12},{10,14},{20,16},{22,... | collective-permute-start | bytes 884744 | tf_op jit(solution)/shard_map/ppermute | solution.py:385
  4.2 14.0 %collective-permute-start.16 = (bf16[768,384]{1,0:T(8,128)(2,1)S(1)}, bf16[768,384]{1,0:T(8,128)(2,1)S(1)}, u32[]{:S(2)}, u32[]{:S(2)}) collective-permute-start(bf16[768,384]{1,0:T(8,128)(2,1)S(1)} %pack.1.refs_2_), channel_id=1, source_target_pairs={{10,2},{12,4},{0,8},{18,10},{20,12},{6,14},{8,16},{26,18},{28,20},... | collective-permute-start | bytes 1769480 | tf_op jit(solution)/shard_map/ppermute | solution.py:385
  7.7 5.7 %collective-permute-start.14 = (bf16[384,384]{1,0:T(8,128)(2,1)S(1)}, bf16[384,384]{1,0:T(8,128)(2,1)S(1)}, u32[]{:S(2)}, u32[]{:S(2)}) collective-permute-start(bf16[384,384]{1,0:T(8,128)(2,1)S(1)} %copy-done.2), channel_id=1, source_target_pairs={{2,0},{0,2},{6,4},{4,6},{10,8},{8,10},{14,12},{12,14},{18,16},{16,... | collective-permute-start | bytes 884744 | tf_op jit(solution)/shard_map/ppermute | solution.py:385
  7.8 13.1 %collective-permute-start.13 = (bf16[768,384]{1,0:T(8,128)(2,1)S(1)}, bf16[768,384]{1,0:T(8,128)(2,1)S(1)}, u32[]{:S(2)}, u32[]{:S(2)}) collective-permute-start(bf16[768,384]{1,0:T(8,128)(2,1)S(1)} %pack.1.refs_2_), channel_id=1, source_target_pairs={{8,0},{14,6},{16,8},{2,10},{4,12},{22,14},{24,16},{10,18},{12,20},... | collective-permute-start | bytes 1769480 | tf_op jit(solution)/shard_map/ppermute | solution.py:385
  10.3 5.2 %collective-permute-start.15 = (bf16[384,384]{1,0:T(8,128)(2,1)S(1)}, bf16[384,384]{1,0:T(8,128)(2,1)S(1)}, u32[]{:S(2)}, u32[]{:S(2)}) collective-permute-start(bf16[384,384]{1,0:T(8,128)(2,1)S(1)} %collective-permute-done.12.refs_0_.refs_2_), channel_id=1, source_target_pairs={{2,0},{0,2},{6,4},{4,6},{10,8},{8,10},{14,12},{12,14},{18,16},{16,... | collective-permute-start | bytes 884744 | tf_op jit(solution)/shard_map/ppermute | solution.py:385
  21.0 17.4 %collective-permute-start.5 = (bf16[768,384]{1,0:T(8,128)(2,1)S(1)}, bf16[768,384]{1,0:T(8,128)(2,1)S(1)}, u32[]{:S(2)}, u32[]{:S(2)}) collective-permute-start(bf16[768,384]{1,0:T(8,128)(2,1)S(1)} %get-tuple-element.116), channel_id=1, source_target_pairs={{8,0},{10,2},{16,8},{18,10},{4,12},{6,14},{24,16},{26,18},{12,20},... | collective-permute-start | bytes 1769480 | tf_op jit(solution)/shard_map/cond/branch_1_fun/ppermute | solution.py:385
  22.4 4.8 %collective-permute-start.6 = (bf16[512,384]{1,0:T(8,128)(2,1)S(1)}, bf16[512,384]{1,0:T(8,128)(2,1)S(1)}, u32[]{:S(2)}, u32[]{:S(2)}) collective-permute-start(bf16[512,384]{1,0:T(8,128)(2,1)S(1)} %corner.1), channel_id=1, source_target_pairs={{12,4},{2,10},{20,12},{10,18},{28,20},{18,26},{13,5},{3,11},{21,13... | collective-permute-start | bytes 1179656 | tf_op jit(solution)/shard_map/cond/branch_1_fun/ppermute | solution.py:385
  39.7 2.3 %collective-permute-start.7 = (f32[392,384]{1,0:T(8,128)S(1)}, f32[392,384]{1,0:T(8,128)S(1)}, u32[]{:S(2)}, u32[]{:S(2)}) collective-permute-start(f32[392,384]{1,0:T(8,128)S(1)} %get-tuple-element.87), channel_id=1, source_target_pairs={{2,0},{0,2},{6,4},{4,6},{10,8},{8,10},{14,12},{12,14},{18,16},{16,... | collective-permute-start | bytes 1806344 | tf_op jit(solution)/shard_map/cond/branch_1_fun/ppermute | solution.py:385
  40.3 2.5 %collective-permute-start.8 = (f32[392,384]{1,0:T(8,128)S(1)}, f32[392,384]{1,0:T(8,128)S(1)}, u32[]{:S(2)}, u32[]{:S(2)}) collective-permute-start(f32[392,384]{1,0:T(8,128)S(1)} %get-tuple-element.89), channel_id=1, source_target_pairs={{2,0},{0,2},{6,4},{4,6},{10,8},{8,10},{14,12},{12,14},{18,16},{16,... | collective-permute-start | bytes 1806344 | tf_op jit(solution)/shard_map/cond/branch_1_fun/ppermute | solution.py:385
  43.4 8.0 %collective-permute-start.9 = (bf16[208,384]{1,0:T(8,128)(2,1)S(1)}, bf16[208,384]{1,0:T(8,128)(2,1)S(1)}, u32[]{:S(2)}, u32[]{:S(2)}) collective-permute-start(bf16[208,384]{1,0:T(8,128)(2,1)S(1)} %get-tuple-element.90), channel_id=1, source_target_pairs={{5,0},{4,1},{7,2},{6,3},{1,4},{0,5},{3,6},{2,7},{13,8},{12,9},{15,... | collective-permute-start | bytes 479240 | tf_op jit(solution)/shard_map/cond/branch_1_fun/ppermute | solution.py:416
  44.9 8.1 %collective-permute-start.10 = (bf16[208,384]{1,0:T(8,128)(2,1)S(1)}, bf16[208,384]{1,0:T(8,128)(2,1)S(1)}, u32[]{:S(2)}, u32[]{:S(2)}) collective-permute-start(bf16[208,384]{1,0:T(8,128)(2,1)S(1)} %get-tuple-element.91), channel_id=1, source_target_pairs={{0,1},{1,0},{2,3},{3,2},{4,5},{5,4},{6,7},{7,6},{8,9},{9,8},{10,11... | collective-permute-start | bytes 479240 | tf_op jit(solution)/shard_map/cond/branch_1_fun/ppermute | solution.py:418
  45.5 8.6 %collective-permute-start.11 = (bf16[208,384]{1,0:T(8,128)(2,1)S(1)}, bf16[208,384]{1,0:T(8,128)(2,1)S(1)}, u32[]{:S(2)}, u32[]{:S(2)}) collective-permute-start(bf16[208,384]{1,0:T(8,128)(2,1)S(1)} %get-tuple-element.92), channel_id=1, source_target_pairs={{4,0},{6,2},{0,4},{2,6},{12,8},{14,10},{8,12},{10,14},{20,16},{22,... | collective-permute-start | bytes 479240 | tf_op jit(solution)/shard_map/cond/branch_1_fun/ppermute | solution.py:385
  55.2 0.7 %copy-start.1 = (bf16[192,768]{1,0:T(8,128)(2,1)}, bf16[192,768]{1,0:T(8,128)(2,1)S(1)}, u32[]{:S(2)}) copy-start(bf16[192,768]{1,0:T(8,128)(2,1)S(1)} %get-tuple-element.147) | copy-start | bytes 884740
